TPU v7x, 512 devices: a whole 4x8x8 slice. The times are simulated.
512 devices in a mesh: dp: 32 (over y_hi, x, core), seq: 16 (over z, y_lo).
Axes of the slice: x: 4, y: 8 (y_hi: 4, y_lo: 2; y = y_hi * 2 + y_lo), z: 8, core: 2. Of those that a mesh axis runs over, the one named last changes fastest.
Arguments:
- query_rows: bfloat16 [32, 2048, 2048], P('dp', 'seq'), may hold values from -108 to 108
- key_rows: bfloat16 [32, 2048, 2048], P('dp', 'seq'), may hold values from -6 to 6
- value_rows: bfloat16 [32, 2048, 2048], P('dp', 'seq'), may hold values from -6 to 6
- out_weight: bfloat16 [2048, 2048], P('seq', 'dp'), may hold values from -0.125 to 0.125
- grad_out: bfloat16 [32, 2048, 2048], P('dp', 'seq'), may hold values from -6 to 6
- block_list: int32 [32, 32, 8], P('dp'), may hold values from 0 to 31, as said below
Outputs:
- attended: bfloat16 [32, 2048, 2048], P('dp', 'seq')
- query_gradient: bfloat16 [32, 2048, 2048], P('dp', 'seq')
- grad_key: bfloat16 [32, 2048, 2048], P('dp', 'seq')
- grad_value: bfloat16 [32, 2048, 2048], P('dp', 'seq')
- grad_weight: float32 [2048, 2048], P('seq', 'dp')
Inputs may be any that keep to these rules, and one draw needn't show every extreme that they name: `block_list`: for query block b, slots 0 to 2 hold b - 1, b, b + 1 modulo 32, slots 3 and 4 hold 0 and 31, slots 5 to 7 are drawn at random; the same list serves all heads.
All inputs are finite; a program needn't handle non-finite values.
Results may differ from a plain program's by a relative error of at most 0.0075.
Values may be sent and summed in bfloat16 or wider, within the bound.
A program may use at most 128 MiB of HBM per device.

v0:
```python
import math

import jax
import jax.numpy as jnp
from jax import lax
from jax.sharding import PartitionSpec as P

HEAD_SIZE = 128


def spread_weight(weight_sum):
    return lax.psum_scatter(weight_sum, "dp", scatter_dimension=1, tiled=True)


def local(query_rows, key_rows, value_rows, out_weight, grad_out, block_list):
    query_all, key_all, value_all = (
        lax.all_to_all(query_rows, "seq", split_axis=2, concat_axis=1, tiled=True),
        lax.all_to_all(key_rows, "seq", split_axis=2, concat_axis=1, tiled=True),
        lax.all_to_all(value_rows, "seq", split_axis=2, concat_axis=1, tiled=True),
    )
    length = query_all.shape[1]
    width_here = query_all.shape[2]
    heads_here = width_here // HEAD_SIZE
    block_ids = block_list[0]
    block_count = block_ids.shape[0]
    slot_count = block_ids.shape[1]
    block_size = length // block_count
    logit_scale = 1.0 / math.sqrt(HEAD_SIZE)

    def to_heads(flat):
        split = flat.reshape(length, heads_here, HEAD_SIZE).transpose(1, 0, 2)
        return split.reshape(heads_here, block_count, block_size, HEAD_SIZE)

    def to_flat(blocked):
        joined = blocked.reshape(heads_here, length, HEAD_SIZE).transpose(1, 0, 2)
        return joined.reshape(1, length, width_here)

    blocked_queries = to_heads(query_all[0])
    key_block_indices = to_heads(key_all[0])[:, block_ids].reshape(
        heads_here, block_count, slot_count * block_size, HEAD_SIZE
    )
    value_block_indices = to_heads(value_all[0])[:, block_ids].reshape(
        heads_here, block_count, slot_count * block_size, HEAD_SIZE
    )
    attention_logits = (
        jnp.einsum(
            "hbqd,hbkd->hbqk",
            blocked_queries,
            key_block_indices,
            preferred_element_type=jnp.float32,
        )
        * logit_scale
    )
    highest = jnp.max(attention_logits, axis=-1, keepdims=True)
    expo = jnp.exp(attention_logits - highest)
    attn_probs = expo / jnp.sum(expo, axis=-1, keepdims=True)
    reduced_probabilities = attn_probs.astype(jnp.bfloat16)
    attended = jnp.einsum(
        "hbqk,hbkd->hbqd",
        reduced_probabilities,
        value_block_indices,
        preferred_element_type=jnp.float32,
    ).astype(jnp.bfloat16)
    attended_flat = to_flat(attended)
    attended_seq = lax.all_to_all(attended_flat, "seq", split_axis=1, concat_axis=2, tiled=True)
    weight_here = lax.all_gather(out_weight, "dp", axis=1, tiled=True)
    gathered_grad = lax.all_gather(grad_out, "seq", axis=1, tiled=True)[0]
    grad_flat = lax.dot_general(
        gathered_grad, weight_here, (((1,), (1,)), ((), ())), preferred_element_type=jnp.float32
    ).astype(jnp.bfloat16)
    weight_sum = lax.dot_general(
        attended_flat[0],
        gathered_grad,
        (((0,), (0,)), ((), ())),
        preferred_element_type=jnp.float32,
    )
    weight_part = None
    gradient_per_block = to_heads(grad_flat)
    value_contributions = jnp.einsum(
        "hbqk,hbqd->hbkd",
        reduced_probabilities,
        gradient_per_block,
        preferred_element_type=jnp.float32,
    )
    probability_gradient = jnp.einsum(
        "hbqd,hbkd->hbqk",
        gradient_per_block,
        value_block_indices,
        preferred_element_type=jnp.float32,
    )
    row_delta = jnp.sum(attn_probs * probability_gradient, axis=-1, keepdims=True)
    score_gradient = (attn_probs * (probability_gradient - row_delta) * logit_scale).astype(
        jnp.bfloat16
    )
    query_gradient = jnp.einsum(
        "hbqk,hbkd->hbqd", score_gradient, key_block_indices, preferred_element_type=jnp.float32
    ).astype(jnp.bfloat16)
    key_contributions = jnp.einsum(
        "hbqk,hbqd->hbkd", score_gradient, blocked_queries, preferred_element_type=jnp.float32
    )
    one_hot = (
        block_ids[:, :, None] == jnp.arange(block_count, dtype=jnp.int32)[None, None, :]
    ).astype(jnp.float32)

    def collect(terms):
        spread = terms.reshape(heads_here, block_count, slot_count, block_size * HEAD_SIZE)
        summed = jnp.einsum(
            "hqsx,qsk->hkx",
            spread,
            one_hot,
            precision=lax.Precision.HIGHEST,
            preferred_element_type=jnp.float32,
        )
        return summed.reshape(heads_here, block_count, block_size, HEAD_SIZE).astype(jnp.bfloat16)

    grad_key = collect(key_contributions)
    grad_value = collect(value_contributions)
    weight_part = spread_weight(weight_sum)
    query_back, key_back, value_back = (
        lax.all_to_all(to_flat(query_gradient), "seq", split_axis=1, concat_axis=2, tiled=True),
        lax.all_to_all(to_flat(grad_key), "seq", split_axis=1, concat_axis=2, tiled=True),
        lax.all_to_all(to_flat(grad_value), "seq", split_axis=1, concat_axis=2, tiled=True),
    )
    return (attended_seq, query_back, key_back, value_back, weight_part)


def solution(mesh):
    return jax.shard_map(
        local,
        mesh=mesh,
        in_specs=(
            P("dp", "seq", None),
            P("dp", "seq", None),
            P("dp", "seq", None),
            P("seq", "dp"),
            P("dp", "seq", None),
            P("dp", None, None),
        ),
        out_specs=(
            P("dp", "seq", None),
            P("dp", "seq", None),
            P("dp", "seq", None),
            P("dp", "seq", None),
            P("seq", "dp"),
        ),
        check_vma=False,
    )
```

profile of v0, /device:TPU:6, one launch (start us, length us, event | category | flops | bytes accessed | tf_op | source)
XLA Modules:
  0.0 453.9 jit_solution(4954409773281861823)
XLA Ops:
  10.8 11.6 %reduce.8 = bf16[2048,128]{1,0:T(8,128)(2,1)S(1)} reduce(bf16[2048,1,128]{2,1,0:T(2,128)(2,1)S(1)} %bitcast.142, bf16[]{:T(256)} %broadcast.67), dimensions={1}, to_apply=%bitcast.91.reduce_sub_computation | reduce | bytes 1048578
  23.3 11.4 %all-to-all-start.1 = ((bf16[16,2,8192]{2,1,0:T(2,128)(2,1)}), bf16[16,2,8192]{2,1,0:T(2,128)(2,1)S(1)}, u32[]{:S(2)}, u32[]{:S(2)}) async-start(bf16[16,2,8192]{2,1,0:T(2,128)(2,1)} %reshape.177), calls=%async_computation.1 | async-start | bytes 1048576 | tf_op jit(solution)/shard_map/all_to_all | solution.py:17
  35.5 11.5 %reduce.7 = bf16[2048,128]{1,0:T(8,128)(2,1)S(1)} reduce(bf16[2048,1,128]{2,1,0:T(2,128)(2,1)S(1)} %bitcast.146, bf16[]{:T(256)} %broadcast.67), dimensions={1}, to_apply=%bitcast.89.reduce_sub_computation | reduce | bytes 1048578
  56.0 14.0 %all-to-all-start = ((bf16[16,2,8192]{2,1,0:T(2,128)(2,1)}), bf16[16,2,8192]{2,1,0:T(2,128)(2,1)S(1)}, u32[]{:S(2)}, u32[]{:S(2)}) async-start(bf16[16,2,8192]{2,1,0:T(2,128)(2,1)} %reshape.175), calls=%async_computation | async-start | bytes 1048576 | tf_op jit(solution)/shard_map/all_to_all | solution.py:18
  70.8 11.5 %reduce.6 = bf16[2048,128]{1,0:T(8,128)(2,1)S(1)} reduce(bf16[2048,1,128]{2,1,0:T(2,128)(2,1)S(1)} %bitcast.147, bf16[]{:T(256)} %broadcast.67), dimensions={1}, to_apply=%bitcast.87.reduce_sub_computation | reduce | bytes 1048578
  94.8 50.7 %all_gather.7 = bf16[128,2048]{0,1:T(8,128)(2,1)} all-gather(bf16[128,64]{0,1:T(8,128)(2,1)S(1)} %copy-done.7), channel_id=1, replica_groups=mesh['dp'=32,'seq'=16] {'dp'}, dimensions={1}, use_global_device_ids=true | all-gather | bytes 540672 | tf_op jit(solution)/shard_map/all_gather | solution.py:66
  164.6 8.1 %copy.135 = bf16[1,2048,128]{2,0,1:T(2,128)(2,1)S(1)} copy(bf16[1,2048,128]{2,1,0:T(8,128)(2,1)S(1)} %bitcast.149) | data formatting | bytes 1048576 | tf_op jit(solution)/shard_map/reshape;transpose;reshape | solution.py:36
  172.7 11.9 %reduce.9 = bf16[2048,128]{1,0:T(8,128)(2,1)S(1)} reduce(bf16[2048,1,128]{2,1,0:T(2,128)(2,1)S(1)} %bitcast.148, bf16[]{:T(256)} %broadcast.67), dimensions={1}, to_apply=%bitcast.124.reduce_sub_computation | reduce | bytes 1048578
  192.7 38.9 %all-gather.2.cloned.1.call-done = bf16[1,2048,2048]{2,1,0:T(8,128)(2,1)} async-done(((bf16[1,128,2048]{2,1,0:T(8,128)(2,1)}), bf16[1,2048,2048]{2,1,0:T(8,128)(2,1)}) %all-gather.2.cloned.1.call-update) | async-done | bytes 8388624 | tf_op jit(solution)/shard_map/all_gather | solution.py:67
  241.1 18.6 %fusion.42 = bf16[32,64,128]{2,1,0:T(8,128)(2,1)S(1)} fusion(bf16[32,512,128]{2,1,0:T(8,128)(2,1)} %bitcast.141, f32[32,64,512]{2,1,0:T(8,128)} %fusion.61, f32[32,64,512]{2,1,0:T(8,128)} %get-tuple-element.26, f32[32,64]{1,0:T(8,128)S(1)} %get-tuple-element.25), kind=kOutput, calls=%fused_computation.34 | convolution fusion | flops 276040192 | bytes 13115392 | tf_op jit(solution)/shard_map/hbqk,hbkd->hbqd/dot_general | solution.py:95
  267.8 11.7 %reduce.10 = bf16[2048,128]{1,0:T(8,128)(2,1)S(1)} reduce(bf16[2048,1,128]{2,1,0:T(2,128)(2,1)S(1)} %bitcast.144, bf16[]{:T(256)} %broadcast.67), dimensions={1}, to_apply=%bitcast.123.reduce_sub_computation | reduce | bytes 1048578
  280.4 8.2 %all-to-all-start.4 = ((bf16[16,2,8192]{2,1,0:T(2,128)(2,1)}), bf16[16,2,8192]{2,1,0:T(2,128)(2,1)S(1)}, u32[]{:S(2)}, u32[]{:S(2)}) async-start(bf16[16,2,8192]{2,1,0:T(2,128)(2,1)} %reshape.181), calls=%async_computation.4 | async-start | bytes 1048576 | tf_op jit(solution)/shard_map/all_to_all | solution.py:120
  296.5 21.3 %fusion.22 = f32[32,512,128]{2,1,0:T(8,128)} fusion(bf16[32,64,128]{2,1,0:T(8,128)(2,1)S(1)} %bitcast.168, f32[32,64,512]{2,1,0:T(8,128)} %fusion.61, f32[32,64,512]{2,1,0:T(8,128)} %get-tuple-element.26, f32[32,64]{1,0:T(8,128)S(1)} %get-tuple-element.25), kind=kOutput, calls=%fused_computation.23 | convolution fusion | flops 275778048 | bytes 17309696 | tf_op jit(solution)/shard_map/hbqk,hbqd->hbkd/dot_general | solution.py:98
  317.8 9.6 %reshape.140 = f32[32,8,8192]{2,1,0:T(8,128)} reshape(f32[32,512,128]{2,1,0:T(8,128)} %fusion.22) | data formatting | bytes 16777216 | tf_op jit(solution)/shard_map/reshape.33
  332.5 8.2 %fusion.39 = bf16[32,64,128]{2,0,1:T(8,128)(2,1)S(1)} fusion(f32[64,128,32,8]{1,0,3,2:T(8,128)S(1)} %bitcast.128, s32[32,8]{0,1:T(8,128)S(1)} %bitcast.169), kind=kOutput, calls=%fused_computation.32 | convolution fusion | flops 805576704 | bytes 8913920 | tf_op jit(solution)/shard_map/hqsx,qsk->hkx/dot_general | solution.py:107
  340.9 8.5 %copy.133 = bf16[1,2048,128]{2,0,1:T(2,128)(2,1)S(1)} copy(bf16[1,2048,128]{2,1,0:T(8,128)(2,1)S(1)} %bitcast.154) | data formatting | bytes 1048576 | tf_op jit(solution)/shard_map/reshape;transpose;reshape | solution.py:36
  349.4 11.5 %reduce.11 = bf16[2048,128]{1,0:T(8,128)(2,1)S(1)} reduce(bf16[2048,1,128]{2,1,0:T(2,128)(2,1)S(1)} %bitcast.145, bf16[]{:T(256)} %broadcast.67), dimensions={1}, to_apply=%bitcast.122.reduce_sub_computation | reduce | bytes 1048578
  361.9 8.3 %all-to-all-start.5 = ((bf16[16,2,8192]{2,1,0:T(2,128)(2,1)}), bf16[16,2,8192]{2,1,0:T(2,128)(2,1)S(1)}, u32[]{:S(2)}, u32[]{:S(2)}) async-start(bf16[16,2,8192]{2,1,0:T(2,128)(2,1)} %reshape.183), calls=%async_computation.5 | async-start | bytes 1048576 | tf_op jit(solution)/shard_map/all_to_all | solution.py:121
  377.3 9.4 %reshape.141 = f32[32,8,8192]{2,1,0:T(8,128)} reshape(f32[32,512,128]{2,1,0:T(8,128)} %fusion.45) | data formatting | bytes 16777216 | tf_op jit(solution)/shard_map/reshape.40
  391.8 8.2 %fusion.36 = bf16[32,64,128]{2,0,1:T(8,128)(2,1)S(1)} fusion(f32[64,128,32,8]{1,0,3,2:T(8,128)S(1)} %bitcast.130, s32[32,8]{0,1:T(8,128)S(1)} %bitcast.170), kind=kOutput, calls=%fused_computation.31 | convolution fusion | flops 805576704 | bytes 8913920 | tf_op jit(solution)/shard_map/hqsx,qsk->hkx/dot_general | solution.py:107
  400.1 8.3 %copy.132 = bf16[1,2048,128]{2,0,1:T(2,128)(2,1)S(1)} copy(bf16[1,2048,128]{2,1,0:T(8,128)(2,1)S(1)} %bitcast.155) | data formatting | bytes 1048576 | tf_op jit(solution)/shard_map/reshape;transpose;reshape | solution.py:36
  408.5 11.5 %reduce.12 = bf16[2048,128]{1,0:T(8,128)(2,1)S(1)} reduce(bf16[2048,1,128]{2,1,0:T(2,128)(2,1)S(1)} %bitcast.143, bf16[]{:T(256)} %broadcast.67), dimensions={1}, to_apply=%bitcast.121.reduce_sub_computation | reduce | bytes 1048578
  420.9 8.2 %all-to-all-start.6 = ((bf16[16,2,8192]{2,1,0:T(2,128)(2,1)}), bf16[16,2,8192]{2,1,0:T(2,128)(2,1)S(1)}, u32[]{:S(2)}, u32[]{:S(2)}) async-start(bf16[16,2,8192]{2,1,0:T(2,128)(2,1)} %reshape.185), calls=%async_computation.6 | async-start | bytes 1048576 | tf_op jit(solution)/shard_map/all_to_all | solution.py:122
  434.9 10.0 %all-to-all-done.6 = bf16[16,2,8192]{2,1,0:T(2,128)(2,1)S(1)} async-done(((bf16[16,2,8192]{2,1,0:T(2,128)(2,1)}), bf16[16,2,8192]{2,1,0:T(2,128)(2,1)S(1)}, u32[]{:S(2)}, u32[]{:S(2)}) %all-to-all-start.6) | async-done | bytes 524320 | tf_op jit(solution)/shard_map/all_to_all | solution.py:122
  (82 shorter events, 107.8 us)
Async XLA Ops:
  7.2 27.6 %copy-start.1 = (bf16[1,128,2048]{2,1,0:T(8,128)(2,1)S(1)}, bf16[1,128,2048]{2,1,0:T(8,128)(2,1)}, u32[]{:S(2)}) copy-start(bf16[1,128,2048]{2,1,0:T(8,128)(2,1)} %param.7) | copy-start | bytes 1572868
  7.2 224.5 %all-gather.2.cloned.1.call-start = ((), (), s32[]{:S(2)}) async-start(), calls=%async_computation.8 | async-start | bytes 8912896 | tf_op jit(solution)/shard_map/all_gather | solution.py:67
  10.8 59.2 %copy-start.2 = (bf16[1,128,2048]{2,1,0:T(8,128)(2,1)S(1)}, bf16[1,128,2048]{2,1,0:T(8,128)(2,1)}, u32[]{:S(2)}) copy-start(bf16[1,128,2048]{2,1,0:T(8,128)(2,1)} %param.8) | copy-start | bytes 1572868
  23.3 32.7 %all-to-all-start.1 = ((bf16[16,2,8192]{2,1,0:T(2,128)(2,1)}), bf16[16,2,8192]{2,1,0:T(2,128)(2,1)S(1)}, u32[]{:S(2)}, u32[]{:S(2)}) async-start(bf16[16,2,8192]{2,1,0:T(2,128)(2,1)} %reshape.177), calls=%async_computation.1 | async-start | bytes 1048576 | tf_op jit(solution)/shard_map/all_to_all | solution.py:17
  35.5 59.0 %copy-start.6 = (s32[1,32,8]{1,2,0:T(8,128)S(1)}, s32[1,32,8]{1,2,0:T(8,128)}, u32[]{:S(2)}) copy-start(s32[1,32,8]{1,2,0:T(8,128)} %param.11) | copy-start | bytes 3076
  35.5 59.2 %copy-start.7 = (bf16[128,64]{0,1:T(8,128)(2,1)S(1)}, bf16[128,64]{0,1:T(8,128)(2,1)}, u32[]{:S(2)}) copy-start(bf16[128,64]{0,1:T(8,128)(2,1)} %param.9) | copy-start | bytes 49156
  56.0 34.9 %all-to-all-start = ((bf16[16,2,8192]{2,1,0:T(2,128)(2,1)}), bf16[16,2,8192]{2,1,0:T(2,128)(2,1)S(1)}, u32[]{:S(2)}, u32[]{:S(2)}) async-start(bf16[16,2,8192]{2,1,0:T(2,128)(2,1)} %reshape.175), calls=%async_computation | async-start | bytes 1048576 | tf_op jit(solution)/shard_map/all_to_all | solution.py:18
  90.8 56.5 %all-to-all-start.2 = ((bf16[16,2,8192]{2,1,0:T(2,128)(2,1)}), bf16[16,2,8192]{2,1,0:T(2,128)(2,1)S(1)}, u32[]{:S(2)}, u32[]{:S(2)}) async-start(bf16[16,2,8192]{2,1,0:T(2,128)(2,1)} %reshape.173), calls=%async_computation.2 | async-start | bytes 1048576 | tf_op jit(solution)/shard_map/all_to_all | solution.py:19
  146.4 8.0 %copy-start.3 = (bf16[1,16,128,128]{3,2,1,0:T(8,128)(2,1)}, bf16[1,16,128,128]{3,2,1,0:T(8,128)(2,1)S(1)}, u32[]{:S(2)}) copy-start(bf16[1,16,128,128]{3,2,1,0:T(8,128)(2,1)S(1)} %copy.82) | copy-start | bytes 1572868
  164.5 67.1 %copy-start.5 = (bf16[128,2048]{0,1:T(8,128)(2,1)S(1)}, bf16[128,2048]{0,1:T(8,128)(2,1)}, u32[]{:S(2)}) copy-start(bf16[128,2048]{0,1:T(8,128)(2,1)} %all_gather.7) | copy-start | bytes 1572868
  185.6 94.9 %all-to-all-start.3 = ((bf16[16,2,8192]{2,1,0:T(2,128)(2,1)}), bf16[16,2,8192]{2,1,0:T(2,128)(2,1)S(1)}, u32[]{:S(2)}, u32[]{:S(2)}) async-start(bf16[16,2,8192]{2,1,0:T(2,128)(2,1)} %reshape.179), calls=%async_computation.3 | async-start | bytes 1048576 | tf_op jit(solution)/shard_map/all_to_all | solution.py:65
  231.7 5.9 %copy-start = (bf16[256,64,128]{2,1,0:T(8,128)(2,1)S(1)}, bf16[256,64,128]{2,1,0:T(8,128)(2,1)}, u32[]{:S(2)}) copy-start(bf16[256,64,128]{2,1,0:T(8,128)(2,1)} %gather_fusion.1) | copy-start | bytes 12582916
  280.4 81.4 %all-to-all-start.4 = ((bf16[16,2,8192]{2,1,0:T(2,128)(2,1)}), bf16[16,2,8192]{2,1,0:T(2,128)(2,1)S(1)}, u32[]{:S(2)}, u32[]{:S(2)}) async-start(bf16[16,2,8192]{2,1,0:T(2,128)(2,1)} %reshape.181), calls=%async_computation.4 | async-start | bytes 1048576 | tf_op jit(solution)/shard_map/all_to_all | solution.py:120
  288.6 158.2 %reduce-scatter.2.cloned.1.call-start = ((), (), s32[]{:S(2)}) async-start(), calls=%async_computation.9 | async-start | bytes 1081344 | tf_op jit(solution)/shard_map/reduce_scatter | solution.py:12
  288.6 7.8 %copy-start.4 = (bf16[1,16,128,128]{3,2,1,0:T(8,128)(2,1)S(1)}, bf16[1,16,128,128]{3,2,1,0:T(8,128)(2,1)}, u32[]{:S(2)}) copy-start(bf16[1,16,128,128]{3,2,1,0:T(8,128)(2,1)} %copy-done.3) | copy-start | bytes 1572868
  361.9 59.1 %all-to-all-start.5 = ((bf16[16,2,8192]{2,1,0:T(2,128)(2,1)}), bf16[16,2,8192]{2,1,0:T(2,128)(2,1)S(1)}, u32[]{:S(2)}, u32[]{:S(2)}) async-start(bf16[16,2,8192]{2,1,0:T(2,128)(2,1)} %reshape.183), calls=%async_computation.5 | async-start | bytes 1048576 | tf_op jit(solution)/shard_map/all_to_all | solution.py:121
  420.9 23.9 %all-to-all-start.6 = ((bf16[16,2,8192]{2,1,0:T(2,128)(2,1)}), bf16[16,2,8192]{2,1,0:T(2,128)(2,1)S(1)}, u32[]{:S(2)}, u32[]{:S(2)}) async-start(bf16[16,2,8192]{2,1,0:T(2,128)(2,1)} %reshape.185), calls=%async_computation.6 | async-start | bytes 1048576 | tf_op jit(solution)/shard_map/all_to_all | solution.py:122
Sparse Core Ops, SparseCore 0:
  10.1 221.5 all-gather.1
  296.6 96.1 reduce-scatter.1
where the time goes:
time: 463 us; the launch traced here: 454 us
  matrix products  90.7 us (20%)
  local copies, waits for them, and re-layouts  90 us (19%)
  other arithmetic  81.4 us (18%)
  waiting for transfers between devices  65.2 us (14%)
  starting transfers between devices  61.1 us (13%)
  blocking collectives  50.7 us (11%)
  between operations  14.7 us (3%)
    unnamed x7, other arithmetic  81.4 us
    all_gather x1, blocking collectives, local(): weight_here = lax.all_gather(out_weight, 'dp', axis=1, tiled=True)  50.7 us
    all_gather x1, waiting for transfers between devices, local(): gathered_grad = lax.all_gather(grad_out, 'seq', axis=1, tiled=True)[0]  38.9 us
    another operation x4, local copies, waits for them, and re-layouts, to_flat(): return joined.reshape(1, length, width_here)  33.2 us
    unnamed x47, local copies, waits for them, and re-layouts  29.2 us
    dot_general x1, matrix products, local(): jnp.einsum('hbqk,hbqd->hbkd', score_gradient, blocked_queries, preferred_...  21.3 us
    another operation x2, local copies, waits for them, and re-layouts  19 us
    dot_general x1, matrix products, local(): jnp.einsum('hbqk,hbkd->hbqd', score_gradient, key_block_indices, preferre...  18.6 us
  transfers between devices with their start and end apart: 9, of which 4 were waited for; matrix products, arithmetic and copies ran while one was open for 58% of the time, Pallas kernels for 0%

commit v1 on v0

v1 whole, which is shorter than its diff:
```python
import functools
import math

import jax
import jax.numpy as jnp
from jax import lax
from jax.experimental import pallas as pl
from jax.experimental.pallas import tpu as pltpu
from jax.sharding import PartitionSpec as P

MESH = pl.DeviceIdType.MESH
F32, BF16 = jnp.float32, jnp.bfloat16
SEQ_LEN, HEADS, HEAD, BLOCK, WIDTH = 2048, 16, 128, 64, 2048
ROWS = SEQ_LEN // 16
NX, NY, NZ = 4, 8, 8
OFFSETS = (0, -1, 1, -2, 2, -3, 3, 4)


class Place:
    def __init__(self):
        self.dp = lax.axis_index("dp")
        self.seq = lax.axis_index("seq")
        self.y_hi = self.dp // 8
        self.x = (self.dp // 2) % 4
        self.core = self.dp % 2
        self.z = self.seq // 2
        self.y_lo = self.seq % 2
        self.y = 2 * self.y_hi + self.y_lo

    def dp_of(self, y_hi=None, x=None, core=None):
        y_hi = self.y_hi if y_hi is None else y_hi
        x = self.x if x is None else x
        core = self.core if core is None else core
        return y_hi * 8 + x * 2 + core

    def at_x(self, x):
        return (self.dp_of(x=x), self.seq)

    def at_y(self, y):
        return (self.dp_of(y_hi=y // 2), 2 * self.z + y % 2)

    def at_z(self, z):
        return (self.dp, 2 * z + self.y_lo)

    def at_seq(self, seq):
        return (self.dp, seq)

    def other_core(self):
        return (self.dp_of(core=1 - self.core), self.seq)


def greet(barrier, place, others):
    def one(d, _):
        to = place.at_seq((place.seq + d) % 16)
        pl.semaphore_signal(barrier, inc=1, device_id=to, device_id_type=MESH)
        return 0

    lax.fori_loop(1, 16, one, 0)
    for to in others:
        pl.semaphore_signal(barrier, inc=1, device_id=to, device_id_type=MESH)
    pl.semaphore_wait(barrier, 15 + len(others))


def remote(src, dst, send, recv, to):
    return pltpu.make_async_remote_copy(
        src_ref=src, dst_ref=dst, send_sem=send, recv_sem=recv, device_id=to, device_id_type=MESH
    )


def each(low, high, act):
    def one(i, _):
        act(i)
        return 0

    lax.fori_loop(low, high, one, 0)


def cols(i):
    return pl.ds(pl.multiple_of(i * HEAD, HEAD), HEAD)


def rows(i):
    return pl.ds(pl.multiple_of(i * ROWS, ROWS), ROWS)


def spread_kernel(
    q_ref, k_ref, v_ref, g_ref, w_ref, qh_ref, kh_ref, vh_ref, dh_ref,
    w_all, d_out, a_send, a_recv, own_sem, z_send, z_recv, y_send, y_recv, x_send, x_recv,
    f_send, f_recv, c_send, c_recv,
):
    here = Place()
    up = here.at_y((here.y + 1) % NY)
    down = here.at_y((here.y + NY - 1) % NY)
    right = here.at_x((here.x + 1) % NX)
    left = here.at_x((here.x + NX - 1) % NX)
    step = 2 * here.y_lo - 1
    far_y = here.at_y((here.y + NY + step) % NY)
    greet(pltpu.get_barrier_semaphore(), here, (far_y, right, left, here.other_core()))

    def moved(src, dst, a, d):
        return remote(
            src.at[:, cols((here.seq + d) % 16)], dst.at[rows(here.seq), :], a_send.at[a, d], a_recv.at[a, d],
            here.at_seq((here.seq + d) % 16),
        )

    def kept(src, dst, a):
        return pltpu.make_async_copy(src.at[:, cols(here.seq)], dst.at[rows(here.seq), :], own_sem.at[a])

    def weights(y, x=None, core=None, z=slice(None)):
        at = pl.multiple_of(here.dp_of(y // 2, x, core) * 64, 64)
        return w_all.at[y % 2, z, pl.ds(at, 64), :]

    own = w_all.at[here.y_lo, here.z, pl.ds(pl.multiple_of(here.dp * 64, 64), 64), :]
    own[...] = w_ref[...].astype(F32).T.astype(BF16)

    def along_z(d):
        return remote(own, own, z_send.at[d], z_recv.at[d], here.at_z((here.z + d) % NZ))

    each(1, NZ, lambda d: along_z(d).start())
    pairs = ((q_ref, qh_ref), (k_ref, kh_ref), (v_ref, vh_ref))
    for a, (src, dst) in enumerate(pairs):
        kept(src, dst, a).start()
        each(1, 16, lambda d: moved(src, dst, a, d).start())
    each(1, NZ, lambda d: along_z(d).wait_recv())

    def along_y(way, k):
        sign = 1 if way == 0 else -1
        half = slice(None) if k < 3 else (pl.ds(0, 4) if way == 0 else pl.ds(4, 4))
        block = weights((here.y - sign * k + NY) % NY, z=half)
        return remote(block, block, y_send.at[way, k], y_recv.at[way, k], up if way == 0 else down)

    def along_x(way, j):
        block = weights((here.y + OFFSETS[j] + NY) % NY)
        return remote(block, block, x_send.at[way, j], x_recv.at[way, j], right if way == 0 else left)

    def from_x(way, j):
        x = (here.x + (NX - 1 if way == 0 else 1)) % NX
        block = weights((here.y + OFFSETS[j] + NY) % NY, x)
        return remote(block, block, f_send.at[j], f_recv.at[j], right if way == 0 else left)

    def to_core(i, j):
        x = (here.x + i) % NX
        block = weights((here.y + OFFSETS[j] + NY) % NY, x)
        return remote(block, block, c_send.at[i, j], c_recv.at[i, j], here.other_core())

    def on(j):
        along_x(0, j).start()
        along_x(1, j).start()
        to_core(0, j).start()

    along_y(0, 0).start()
    along_y(1, 0).start()
    on(0)
    for k in range(3):
        for way in range(2):
            along_y(way, k).wait_recv()
            along_y(way, k + 1).start()
            on(1 + 2 * k + way)
    along_y(0, 3).wait_recv()
    along_y(1, 3).wait_recv()
    on(7)
    for j in range(8):
        for way in range(2):
            along_x(way, j).wait_recv()
            if j % 2 == way:
                from_x(way, j).start()
            to_core(3 if way == 0 else 1, j).start()
    for j in range(8):
        from_x(j % 2, j).wait_recv()
        to_core(2, j).start()
    for i in (0, 3, 1, 2):
        for j in range(8):
            to_core(i, j).wait_recv()

    def project(d):
        head = (here.seq + d) % 16
        w = w_all[head % 2, head // 2]
        d_out[head] = jnp.dot(g_ref[...], w, preferred_element_type=F32).astype(BF16)

    def sent(d):
        head = (here.seq + d) % 16
        return remote(
            d_out.at[head], dh_ref.at[rows(here.seq), :], a_send.at[3, d], a_recv.at[3, d], here.at_seq(head)
        )

    def project_and_send(d):
        project(d)
        sent(d).start()

    each(1, 16, project_and_send)
    project(0)
    own_d = pltpu.make_async_copy(d_out.at[here.seq], dh_ref.at[rows(here.seq), :], own_sem.at[3])
    own_d.start()

    for a, (src, dst) in enumerate(pairs):
        kept(src, dst, a).wait()
        each(1, 16, lambda d: moved(src, dst, a, d).wait())
    own_d.wait()
    each(1, 16, lambda d: sent(d).wait())
    each(1, NZ, lambda d: along_z(d).wait_send())
    for way in range(2):
        for k in range(4):
            along_y(way, k).wait_send()
        for j in range(8):
            along_x(way, j).wait_send()
    for j in range(8):
        from_x(j % 2, j).wait_send()
        for i in range(4):
            to_core(i, j).wait_send()


def spread(q, k, v, g, w):
    flat = jax.ShapeDtypeStruct((SEQ_LEN, HEAD), BF16)
    any_, vmem = pl.BlockSpec(memory_space=pl.ANY), pl.BlockSpec(memory_space=pltpu.VMEM)
    dma = pltpu.SemaphoreType.DMA
    return pl.pallas_call(
        spread_kernel,
        out_shape=(flat,) * 4,
        in_specs=[any_, any_, any_, vmem, vmem],
        out_specs=(any_,) * 4,
        scratch_shapes=[
            pltpu.VMEM((2, NZ, WIDTH, HEAD), BF16),
            pltpu.VMEM((HEADS, ROWS, HEAD), BF16),
            dma((4, 16)), dma((4, 16)), dma((4,)), dma((NZ,)), dma((NZ,)), dma((2, 4)), dma((2, 4)),
            dma((2, 8)), dma((2, 8)), dma((8,)), dma((8,)), dma((4, 8)), dma((4, 8)),
        ],
        compiler_params=pltpu.CompilerParams(
            collective_id=0, has_side_effects=True, vmem_limit_bytes=40 * 2**20
        ),
        name="spread",
    )(q, k, v, g, w)


def attention_kernel(ids_ref, q_ref, k_ref, v_ref, d_ref, att_ref, dq_ref, dk_ref, dv_ref, dk_sum, dv_sum):
    scale = 1.0 / math.sqrt(HEAD)
    slots = ids_ref.shape[1]
    dk_sum[...] = jnp.zeros_like(dk_sum)
    dv_sum[...] = jnp.zeros_like(dv_sum)

    def dot(a, b, i, j):
        return lax.dot_general(a, b, (((i,), (j,)), ((), ())), preferred_element_type=F32)

    def one(b):
        here = pl.ds(pl.multiple_of(b * BLOCK, BLOCK), BLOCK)
        at = [pl.ds(pl.multiple_of(ids_ref[b, s] * BLOCK, BLOCK), BLOCK) for s in range(slots)]
        q, d = q_ref[here, :], d_ref[here, :]
        k = jnp.concatenate([k_ref[i, :] for i in at], axis=0)
        v = jnp.concatenate([v_ref[i, :] for i in at], axis=0)
        logits = dot(q, k, 1, 1) * scale
        expo = jnp.exp(logits - jnp.max(logits, axis=1, keepdims=True))
        probs = expo / jnp.sum(expo, axis=1, keepdims=True)
        low = probs.astype(BF16)
        att_ref[here, :] = dot(low, v, 1, 0).astype(BF16)
        d_probs = dot(d, v, 1, 1)
        delta = jnp.sum(probs * d_probs, axis=1, keepdims=True)
        d_logits = (probs * (d_probs - delta) * scale).astype(BF16)
        dq_ref[here, :] = dot(d_logits, k, 1, 0).astype(BF16)
        dk, dv = dot(d_logits, q, 0, 0), dot(low, d, 0, 0)
        for s in range(slots):
            dk_sum[at[s], :] += dk[s * BLOCK : (s + 1) * BLOCK]
            dv_sum[at[s], :] += dv[s * BLOCK : (s + 1) * BLOCK]

    each(0, SEQ_LEN // BLOCK, one)
    dk_ref[...] = dk_sum[...].astype(BF16)
    dv_ref[...] = dv_sum[...].astype(BF16)


def attention(ids, q, k, v, d):
    flat = jax.ShapeDtypeStruct((SEQ_LEN, HEAD), BF16)
    vmem = pl.BlockSpec(memory_space=pltpu.VMEM)
    return pl.pallas_call(
        attention_kernel,
        out_shape=(flat,) * 4,
        in_specs=[pl.BlockSpec(memory_space=pltpu.SMEM)] + [vmem] * 4,
        out_specs=(vmem,) * 4,
        scratch_shapes=[pltpu.VMEM((SEQ_LEN, HEAD), F32)] * 2,
        compiler_params=pltpu.CompilerParams(vmem_limit_bytes=40 * 2**20),
        name="attention",
    )(ids, q, k, v, d)


def collect_kernel(
    ah_ref, qh_ref, kh_ref, vh_ref, g_ref, att_ref, dq_ref, dk_ref, dv_ref, gw_ref,
    att4, g4, product, c_out, c_in, y_out, y_in, z_out, z_in, last_out, last_in,
    a_send, a_recv, own_sem, g_send, g_recv, x_send, x_recv, f_send, f_recv, c_send, c_recv,
    y_send, y_recv, z_send, z_recv, att_sem,
):
    here = Place()
    right = here.at_x((here.x + 1) % NX)
    left = here.at_x((here.x + NX - 1) % NX)
    others = [here.at_x((here.x + d) % NX) for d in range(1, NX)]
    for d in range(1, 4):
        for y_lo in range(2):
            others.append((here.dp_of(y_hi=(here.y_hi + d) % 4), 2 * here.z + y_lo))
    others.append(here.other_core())
    greet(pltpu.get_barrier_semaphore(), here, others)

    mine = att4.at[here.x]

    def moved(src, dst, a, d):
        to = (here.seq + d) % 16
        return remote(
            src.at[rows(to), :], dst.at[:, cols(here.seq)], a_send.at[a, d], a_recv.at[a, d], here.at_seq(to)
        )

    def kept(src, dst, a):
        return pltpu.make_async_copy(src.at[rows(here.seq), :], dst.at[:, cols(here.seq)], own_sem.at[a])

    def grads(d, y_hi):
        x = (here.x + d) % NX
        return remote(
            g_ref.at[:, cols(y_hi * NX + x)], g4.at[here.x, :, cols(y_hi)], g_send.at[d, y_hi], g_recv.at[d, y_hi],
            here.at_x(x),
        )

    def own_grads(y_hi):
        return pltpu.make_async_copy(
            g_ref.at[:, cols(y_hi * NX + here.x)], g4.at[here.x, :, cols(y_hi)], g_send.at[0, y_hi]
        )

    pairs = ((ah_ref, mine), (qh_ref, dq_ref), (kh_ref, dk_ref), (vh_ref, dv_ref))
    for a, (src, dst) in enumerate(pairs):
        kept(src, dst, a).start()
        each(1, 16, lambda d: moved(src, dst, a, d).start())
        if a == 0:
            for y_hi in range(4):
                own_grads(y_hi).start()
                each(1, NX, lambda d: grads(d, y_hi).start())

    kept(ah_ref, mine, 0).wait()
    each(1, 16, lambda d: moved(ah_ref, mine, 0, d).wait_recv())
    att_copy = pltpu.make_async_copy(mine, att_ref, att_sem)
    att_copy.start()

    def half(part, x):
        return att4.at[x, :, pl.ds(part * (WIDTH // 2), WIDTH // 2)]

    def along_x(way, part):
        block = half(part, here.x)
        return remote(block, block, x_send.at[way, part], x_recv.at[way, part], right if way == 0 else left)

    def forward(way):
        block = half(way, (here.x + (NX - 1 if way == 0 else 1)) % NX)
        return remote(block, block, f_send.at[way], f_recv.at[way], right if way == 0 else left)

    for part in range(2):
        along_x(0, part).start()
        along_x(1, 1 - part).start()
    for way in range(2):
        along_x(way, way).wait_recv()
        forward(way).start()
    for way in range(2):
        along_x(way, 1 - way).wait_recv()
    for way in range(2):
        forward(way).wait_recv()
    for y_hi in range(4):
        own_grads(y_hi).wait()
        each(1, NX, lambda d: grads(d, y_hi).wait_recv())

    def multiply(h):
        a = att4[:, :, cols(h)].reshape(NX * ROWS, HEAD)
        total = lax.dot_general(
            a, g4[...].reshape(NX * ROWS, 4 * HEAD), (((0,), (0,)), ((), ())), preferred_element_type=F32
        )
        product[h] = total
        c_out[h] = total.astype(BF16)

    each(0, HEADS, multiply)

    def half_rows(core):
        return pl.ds(pl.multiple_of(core * 64, 64), 64)

    to_core = remote(
        c_out.at[:, half_rows(1 - here.core), :], c_in, c_send.at[0], c_recv.at[0], here.other_core()
    )
    to_core.start()
    to_core.wait()

    def add_core(h):
        total = product[h, half_rows(here.core), :] + c_in[h].astype(F32)
        for y_hi in range(4):
            y_out[y_hi * 2 + h % 2, h // 2] = total[:, y_hi * HEAD : (y_hi + 1) * HEAD].astype(BF16)

    each(0, HEADS, add_core)

    def along_y(d):
        y = (here.y + d) % NY
        return remote(y_out.at[y], y_in.at[d], y_send.at[d], y_recv.at[d], here.at_y(y))

    each(1, NY, lambda d: along_y(d).start())
    each(1, NY, lambda d: along_y(d).wait())

    def add_y(z):
        total = y_out[here.y, z].astype(F32)
        for d in range(1, NY):
            total += y_in[d, z].astype(F32)
        z_out[z] = total.astype(BF16)

    each(0, NZ, add_y)

    def along_z(d):
        z = (here.z + d) % NZ
        return remote(z_out.at[z], z_in.at[d], z_send.at[d], z_recv.at[d], here.at_z(z))

    each(1, NZ, lambda d: along_z(d).start())
    each(1, NZ, lambda d: along_z(d).wait())
    total = z_out[here.z].astype(F32)
    for d in range(1, NZ):
        total += z_in[d].astype(F32)
    last_out[...] = total
    swap = remote(last_out, last_in, c_send.at[1], c_recv.at[1], here.other_core())
    swap.start()
    swap.wait()
    first = here.core == 0
    top = jnp.where(first, last_out[...], last_in[...])
    bottom = jnp.where(first, last_in[...], last_out[...])
    gw_ref[:64, :] = jnp.where(first, top[:, :64], top[:, 64:])
    gw_ref[64:, :] = jnp.where(first, bottom[:, :64], bottom[:, 64:])

    att_copy.wait()
    for way in range(2):
        for part in range(2):
            along_x(way, part).wait_send()
        forward(way).wait_send()
    for y_hi in range(4):
        each(1, NX, lambda d: grads(d, y_hi).wait_send())
    each(1, 16, lambda d: moved(ah_ref, mine, 0, d).wait_send())
    for a, (src, dst) in enumerate(pairs):
        if a > 0:
            kept(src, dst, a).wait()
            each(1, 16, lambda d: moved(src, dst, a, d).wait())


def collect(att, dq, dk, dv, g):
    flat = jax.ShapeDtypeStruct((ROWS, WIDTH), BF16)
    any_, vmem = pl.BlockSpec(memory_space=pl.ANY), pl.BlockSpec(memory_space=pltpu.VMEM)
    dma = pltpu.SemaphoreType.DMA
    return pl.pallas_call(
        collect_kernel,
        out_shape=(flat,) * 4 + (jax.ShapeDtypeStruct((HEAD, 64), F32),),
        in_specs=[any_] * 5,
        out_specs=(any_,) * 4 + (vmem,),
        scratch_shapes=[
            pltpu.VMEM((NX, ROWS, WIDTH), BF16),
            pltpu.VMEM((NX, ROWS, 4 * HEAD), BF16),
            pltpu.VMEM((HEADS, HEAD, 4 * HEAD), F32),
            pltpu.VMEM((HEADS, HEAD, 4 * HEAD), BF16),
            pltpu.VMEM((HEADS, 64, 4 * HEAD), BF16),
            pltpu.VMEM((NY, NZ, 64, HEAD), BF16),
            pltpu.VMEM((NY, NZ, 64, HEAD), BF16),
            pltpu.VMEM((NZ, 64, HEAD), BF16),
            pltpu.VMEM((NZ, 64, HEAD), BF16),
            pltpu.VMEM((64, HEAD), F32),
            pltpu.VMEM((64, HEAD), F32),
            dma((4, 16)), dma((4, 16)), dma((4,)), dma((4, 4)), dma((4, 4)), dma((2, 2)), dma((2, 2)),
            dma((2,)), dma((2,)), dma((2,)), dma((2,)), dma((NY,)), dma((NY,)), dma((NZ,)), dma((NZ,)),
            dma,
        ],
        compiler_params=pltpu.CompilerParams(
            collective_id=1, has_side_effects=True, vmem_limit_bytes=40 * 2**20
        ),
        name="collect",
    )(att, dq, dk, dv, g)


def local(query_rows, key_rows, value_rows, out_weight, grad_out, block_list):
    heads = spread(query_rows[0], key_rows[0], value_rows[0], grad_out[0], out_weight)
    results = attention(block_list[0], *heads)
    att, dq, dk, dv, grad_weight = collect(*results, grad_out[0])
    return (att[None], dq[None], dk[None], dv[None], grad_weight)


def solution(mesh):
    return jax.shard_map(
        local,
        mesh=mesh,
        in_specs=(
            P("dp", "seq", None),
            P("dp", "seq", None),
            P("dp", "seq", None),
            P("seq", "dp"),
            P("dp", "seq", None),
            P("dp", None, None),
        ),
        out_specs=(
            P("dp", "seq", None),
            P("dp", "seq", None),
            P("dp", "seq", None),
            P("dp", "seq", None),
            P("seq", "dp"),
        ),
        check_vma=False,
    )
```

time: 463 us -> 232 us (0.50); the launches traced: 454 us -> 231 us
  Pallas kernels: 0 us -> 222 us
  matrix products: 90.7 us -> 0 us
  other arithmetic: 81.4 us -> 0 us
  local copies, waits for them, and re-layouts: 90 us -> 8.91 us
  waiting for transfers between devices: 65.2 us -> 0 us
  starting transfers between devices: 61.1 us -> 0 us
  blocking collectives: 50.7 us -> 0 us
  between operations: 14.7 us -> 0.7 us
    pallas_call x0 -> x3, Pallas kernels: none -> 222 us  [the longest x1 102 us: collect(): pl.pallas_call(collect_kernel, out_shape=(flat,) * 4 + (jax.ShapeDtypeStr...]
    dot_general x9 -> x0, matrix products: 84.9 us -> none  [the longest x1 21.3 us: local(): jnp.einsum('hbqk,hbqd->hbkd', score_gradient, blocked_queries, preferred_...]
    unnamed x7 -> x0, other arithmetic: 81.4 us -> none
    all_to_all x7 -> x0, starting transfers between devices: 61 us -> none  [the longest x1 14 us: local(): lax.all_to_all(key_rows, 'seq', split_axis=2, concat_axis=1, tiled=True)]
    another operation x6 -> x0, local copies, waits for them, and re-layouts: 52.2 us -> none  [the longest x4 33.2 us: to_flat(): return joined.reshape(1, length, width_here)]
    all_gather x1 -> x0, blocking collectives: 50.7 us -> none  [local(): weight_here = lax.all_gather(out_weight, 'dp', axis=1, tiled=True)]
    all_gather x1 -> x0, waiting for transfers between devices: 38.9 us -> none  [local(): gathered_grad = lax.all_gather(grad_out, 'seq', axis=1, tiled=True)[0]]
    all_to_all x7 -> x0, waiting for transfers between devices: 25.5 us -> none  [the longest x1 9.98 us: local(): lax.all_to_all(to_flat(grad_value), 'seq', split_axis=1, concat_axis=2, t...]
  transfers between devices with their start and end apart: 9 -> 0, of which waited for: 4 -> 0; matrix products, arithmetic and copies ran while one was open for 58% -> 0% of each run, Pallas kernels for 0% -> 0%
where the time goes in v1:
time: 232 us; the launch traced here: 231 us
  Pallas kernels  222 us (96%)
  local copies, waits for them, and re-layouts  8.91 us (4%)
    pallas_call x1, Pallas kernels, collect(): pl.pallas_call(collect_kernel, out_shape=(flat,) * 4 + (jax.ShapeDtypeStr...  102 us
    pallas_call x1, Pallas kernels, spread(): pl.pallas_call(spread_kernel, out_shape=(flat,) * 4, in_specs=[any_, any_...  91.6 us
    pallas_call x1, Pallas kernels, attention(): pl.pallas_call(attention_kernel, out_shape=(flat,) * 4, in_specs=[pl.Bloc...  28.1 us
    unnamed x21, local copies, waits for them, and re-layouts  8.91 us

profile of v1, /device:TPU:6, one launch (start us, length us, event | category | flops | bytes accessed | tf_op | source)
XLA Modules:
  0.0 231.3 jit_solution(14601409681873872954)
XLA Ops:
  0.6 0.0 copy-start.6
  0.6 0.0 copy-start.5
  0.7 0.7 copy-done.6
  1.3 0.1 copy.11
  1.4 0.0 copy-done.5
  1.4 0.1 copy.12.w_ref
  1.5 0.0 copy-start
  1.5 1.0 copy-done
  2.6 0.0 copy-start.2
  2.6 1.0 copy-done.2
  3.6 0.0 copy-start.3
  3.6 1.0 copy-done.3
  4.7 0.0 copy-start.4
  4.7 1.0 copy-done.4
  5.7 91.6 %spread.1 = (bf16[2048,128]{1,0:T(8,128)(2,1)S(1)}, bf16[2048,128]{1,0:T(8,128)(2,1)S(1)}, bf16[2048,128]{1,0:T(8,128)(2,1)S(1)}, bf16[2048,128]{1,0:T(8,128)(2,1)S(1)}) custom-call(bf16[128,2048]{1,0:T(8,128)(2,1)S(1)} %bitcast.15, bf16[128,2048]{1,0:T(8,128)(2,1)S(1)} %bitcast.16, bf16[128,2048]{1,0:T(8,128)(2,1)S(1)} %bitcast.17, ...), custom_call_target="tpu_custom_call" | custom-call | tf_op jit(solution)/shard_map/spread/pallas_call | solution.py:216
  97.3 0.0 copy-start.1
  97.3 28.1 %attention.1 = (bf16[2048,128]{1,0:T(8,128)(2,1)S(1)}, bf16[2048,128]{1,0:T(8,128)(2,1)S(1)}, bf16[2048,128]{1,0:T(8,128)(2,1)S(1)}, bf16[2048,128]{1,0:T(8,128)(2,1)S(1)}) custom-call(s32[32,8]{1,0:T(8,128)S(1)} %bitcast.18, bf16[2048,128]{1,0:T(8,128)(2,1)S(1)} %get-tuple-element.18.q_ref, bf16[2048,128]{1,0:T(8,128)(2,1)S(1)} %get-tuple-element.19.k_ref, ...), custom_call_target="tpu_custom_call" | custom-call | tf_op jit(solution)/shard_map/attention/pallas_call | solution.py:271
  125.5 0.0 copy-done.1
  125.5 102.0 %collect.1 = (bf16[128,2048]{1,0:T(8,128)(2,1)S(1)}, bf16[128,2048]{1,0:T(8,128)(2,1)S(1)}, bf16[128,2048]{1,0:T(8,128)(2,1)S(1)}, bf16[128,2048]{1,0:T(8,128)(2,1)S(1)}, f32[128,64]{1,0:T(8,128)S(1)}) custom-call(bf16[2048,128]{1,0:T(8,128)(2,1)S(1)} %get-tuple-element.22.ah_ref, bf16[2048,128]{1,0:T(8,128)(2,1)S(1)} %get-tuple-element.23.qh_ref, ...), custom_call_target="tpu_custom_call" | custom-call | tf_op jit(solution)/shard_map/collect/pallas_call | solution.py:438
  227.5 0.7 copy.13
  228.2 0.8 copy.18
  229.0 0.8 copy.19
  229.8 0.8 copy.20
  230.5 0.8 copy.21
Async XLA Ops:
  0.6 0.7 copy-start.6
  0.6 0.8 copy-start.5
  1.5 1.1 copy-start
  2.6 1.0 copy-start.2
  3.6 1.0 copy-start.3
  4.7 1.0 copy-start.4
  97.3 28.1 %copy-start.1 = (bf16[1,128,2048]{2,1,0:T(8,128)(2,1)S(1)}, bf16[1,128,2048]{2,1,0:T(8,128)(2,1)}, u32[]{:S(2)}) copy-start(bf16[1,128,2048]{2,1,0:T(8,128)(2,1)} %param.10) | copy-start | bytes 1572868

commit v2 on v1

v2 whole, which is shorter than its diff:
```python
import functools
import math

import jax
import jax.numpy as jnp
from jax import lax
from jax.experimental import pallas as pl
from jax.experimental.pallas import tpu as pltpu
from jax.sharding import PartitionSpec as P

MESH = pl.DeviceIdType.MESH
F32, BF16 = jnp.float32, jnp.bfloat16
SEQ_LEN, HEADS, HEAD, BLOCK, WIDTH = 2048, 16, 128, 64, 2048
ROWS = SEQ_LEN // 16
NX, NY, NZ = 4, 8, 8
OFFSETS = (0, -1, 1, -2, 2, -3, 3, 4)


SAME_Y, OTHER_Y = (8, 6, 10, 4, 12, 2, 14), (7, 9, 5, 11, 3, 13, 1, 15)


class Queue:
    def __init__(self, copies):
        self.copies = list(copies)

    def start(self, count):
        for make, *args in self.copies[:count]:
            make(*args).start()
        self.copies = self.copies[count:]


class Place:
    def __init__(self):
        self.dp = lax.axis_index("dp")
        self.seq = lax.axis_index("seq")
        self.y_hi = self.dp // 8
        self.x = (self.dp // 2) % 4
        self.core = self.dp % 2
        self.z = self.seq // 2
        self.y_lo = self.seq % 2
        self.y = 2 * self.y_hi + self.y_lo

    def dp_of(self, y_hi=None, x=None, core=None):
        y_hi = self.y_hi if y_hi is None else y_hi
        x = self.x if x is None else x
        core = self.core if core is None else core
        return y_hi * 8 + x * 2 + core

    def at_x(self, x):
        return (self.dp_of(x=x), self.seq)

    def at_y(self, y):
        return (self.dp_of(y_hi=y // 2), 2 * self.z + y % 2)

    def at_z(self, z):
        return (self.dp, 2 * z + self.y_lo)

    def at_seq(self, seq):
        return (self.dp, seq)

    def other_core(self):
        return (self.dp_of(core=1 - self.core), self.seq)


def greet(barrier, place, others):
    def one(d, _):
        to = place.at_seq((place.seq + d) % 16)
        pl.semaphore_signal(barrier, inc=1, device_id=to, device_id_type=MESH)
        return 0

    lax.fori_loop(1, 16, one, 0)
    for to in others:
        pl.semaphore_signal(barrier, inc=1, device_id=to, device_id_type=MESH)
    pl.semaphore_wait(barrier, 15 + len(others))


def remote(src, dst, send, recv, to):
    return pltpu.make_async_remote_copy(
        src_ref=src, dst_ref=dst, send_sem=send, recv_sem=recv, device_id=to, device_id_type=MESH
    )


def each(low, high, act):
    def one(i, _):
        act(i)
        return 0

    lax.fori_loop(low, high, one, 0)


def cols(i):
    return pl.ds(pl.multiple_of(i * HEAD, HEAD), HEAD)


def rows(i):
    return pl.ds(pl.multiple_of(i * ROWS, ROWS), ROWS)


def dot(a, b, i, j):
    return lax.dot_general(a, b, (((i,), (j,)), ((), ())), preferred_element_type=F32)


def block(b):
    return pl.ds(pl.multiple_of(b * BLOCK, BLOCK), BLOCK)


SLOTS = 8
SCALE = 1.0 / math.sqrt(HEAD)
TOGETHER = 4


def listed(ids_ref, b):
    return [ids_ref[b, s] for s in range(SLOTS)]


def gathered(ref, at):
    return jnp.concatenate([ref[i] for i in at], axis=0)


FLAT = jax.ShapeDtypeStruct((SEQ_LEN, HEAD), BF16)
BLOCKED = jax.ShapeDtypeStruct((SEQ_LEN // BLOCK, BLOCK, HEAD), BF16)
PROBS = jax.ShapeDtypeStruct((SEQ_LEN // BLOCK, BLOCK, SLOTS * BLOCK), F32)
VMEM = pl.BlockSpec(memory_space=pltpu.VMEM)


def outward_kernel(
    ids_ref, q_ref, k_ref, v_ref, g_ref, w_ref, qh_ref, kh_ref, vh_ref, dh_ref, probs_ref, att_ref, att4, g4,
    w_all, att_out, d_out, a_send, a_recv, own_sem, z_send, z_recv, y_send, y_recv, x_send, x_recv,
    f_send, f_recv, c_send, c_recv, g_send, g_recv, m_send, m_recv, n_send, n_recv,
):
    here = Place()
    up = here.at_y((here.y + 1) % NY)
    down = here.at_y((here.y + NY - 1) % NY)
    right = here.at_x((here.x + 1) % NX)
    left = here.at_x((here.x + NX - 1) % NX)
    far_y = here.at_y((here.y + NY + 2 * here.y_lo - 1) % NY)
    others = [here.at_x((here.x + d) % NX) for d in range(1, NX)]
    greet(pltpu.get_barrier_semaphore(), here, [far_y, here.other_core()] + others)
    mine = att4.at[here.x]

    def seq_at(d):
        return (here.seq + d) % 16

    def moved(src, dst, a, d):
        return remote(
            src.at[:, :, cols(seq_at(d))], dst.at[pl.ds(2 * here.seq, 2)], a_send.at[a, d], a_recv.at[a, d],
            here.at_seq(seq_at(d)),
        )

    def kept(src, dst, a):
        return pltpu.make_async_copy(src.at[:, :, cols(here.seq)], dst.at[pl.ds(2 * here.seq, 2)], own_sem.at[a])

    def arrived(src, dst, a):
        kept(src, dst, a).wait()
        each(1, 16, lambda d: moved(src, dst, a, d).wait_recv())

    def weights(y, x=None, z=slice(None)):
        at = pl.multiple_of(here.dp_of(y // 2, x) * 64, 64)
        return w_all.at[y % 2, z, pl.ds(at, 64), :]

    own = w_all.at[here.y_lo, here.z, pl.ds(pl.multiple_of(here.dp * 64, 64), 64), :]
    own[...] = w_ref[...].astype(F32).T.astype(BF16)

    def along_z(d):
        return remote(own, own, z_send.at[d], z_recv.at[d], here.at_z((here.z + d) % NZ))

    def along_y(way, k):
        sign = 1 if way == 0 else -1
        part = slice(None) if k < 3 else (pl.ds(0, 4) if way == 0 else pl.ds(4, 4))
        at = weights((here.y - sign * k + NY) % NY, z=part)
        return remote(at, at, y_send.at[way, k], y_recv.at[way, k], up if way == 0 else down)

    def along_x(way, j):
        at = weights((here.y + OFFSETS[j] + NY) % NY)
        return remote(at, at, x_send.at[way, j], x_recv.at[way, j], right if way == 0 else left)

    def from_x(way, j):
        x = (here.x + (NX - 1 if way == 0 else 1)) % NX
        at = weights((here.y + OFFSETS[j] + NY) % NY, x)
        return remote(at, at, f_send.at[j], f_recv.at[j], right if way == 0 else left)

    def to_core(i, j):
        at = weights((here.y + OFFSETS[j] + NY) % NY, (here.x + i) % NX)
        return remote(at, at, c_send.at[i, j], c_recv.at[i, j], here.other_core())

    def on(j):
        along_x(0, j).start()
        along_x(1, j).start()
        to_core(0, j).start()

    def grads(d, y_hi):
        x = (here.x + d) % NX
        return remote(
            g_ref.at[:, cols(y_hi * NX + x)], g4.at[here.x, :, cols(y_hi)], g_send.at[d, y_hi], g_recv.at[d, y_hi],
            here.at_x(x),
        )

    def own_grads(y_hi):
        return pltpu.make_async_copy(
            g_ref.at[:, cols(y_hi * NX + here.x)], g4.at[here.x, :, cols(y_hi)], g_send.at[0, y_hi]
        )

    def att(d):
        to = seq_at(d)
        return remote(
            att_out.at[rows(to), :], mine.at[:, cols(here.seq)], a_send.at[3, d], a_recv.at[3, d], here.at_seq(to)
        )

    own_att = pltpu.make_async_copy(att_out.at[rows(here.seq), :], mine.at[:, cols(here.seq)], own_sem.at[3])

    def d_att(d):
        to = seq_at(d)
        return remote(d_out.at[to], dh_ref.at[rows(here.seq), :], a_send.at[4, d], a_recv.at[4, d], here.at_seq(to))

    own_d = pltpu.make_async_copy(d_out.at[here.seq], dh_ref.at[rows(here.seq), :], own_sem.at[4])

    def half(part, x):
        return att4.at[x, :, pl.ds(part * (WIDTH // 2), WIDTH // 2)]

    def att_x(way, part):
        at = half(part, here.x)
        return remote(at, at, m_send.at[way, part], m_recv.at[way, part], right if way == 0 else left)

    def att_onward(way):
        at = half(way, (here.x + (NX - 1 if way == 0 else 1)) % NX)
        return remote(at, at, n_send.at[way], n_recv.at[way], right if way == 0 else left)

    pairs = ((q_ref, qh_ref), (k_ref, kh_ref), (v_ref, vh_ref))
    order = [(0, SAME_Y), (1, SAME_Y), (0, OTHER_Y), (1, OTHER_Y), (2, SAME_Y), (2, OTHER_Y)]
    queue = Queue((moved, *pairs[a], a, d) for a, ds in order for d in ds)
    each(1, NZ, lambda d: along_z(d).start())
    queue.start(14)
    for a, (src, dst) in enumerate(pairs):
        kept(src, dst, a).start()
    each(1, NZ, lambda d: along_z(d).wait_recv())
    along_y(0, 0).start()
    along_y(1, 0).start()
    on(0)
    for k in range(3):
        for way in range(2):
            along_y(way, k).wait_recv()
            along_y(way, k + 1).start()
            on(1 + 2 * k + way)
            queue.start(3)
    along_y(0, 3).wait_recv()
    along_y(1, 3).wait_recv()
    on(7)

    def next_x(j):
        for way in range(2):
            along_x(way, j).wait_recv()
            if j % 2 == way:
                from_x(way, j).start()
            queue.start(2)
            to_core(3 if way == 0 else 1, j).start()

    for j in range(4):
        next_x(j)

    arrived(*pairs[0], 0)
    arrived(*pairs[1], 1)

    def softmax(step):
        blocks = [step * TOGETHER + i for i in range(TOGETHER)]
        logits = [dot(qh_ref[b], gathered(kh_ref, listed(ids_ref, b)), 1, 1) * SCALE for b in blocks]
        expo = [jnp.exp(x - jnp.max(x, axis=1, keepdims=True)) for x in logits]
        for b, x in zip(blocks, expo):
            probs_ref[b] = x / jnp.sum(x, axis=1, keepdims=True)

    steps = SEQ_LEN // BLOCK // TOGETHER // 4
    for j in range(4):
        each(j * steps, (j + 1) * steps, softmax)
        next_x(4 + j)
    arrived(*pairs[2], 2)

    def attend(chunks):
        blocks = [2 * c + i for c in chunks for i in range(2)]
        out = [dot(probs_ref[b].astype(BF16), gathered(vh_ref, listed(ids_ref, b)), 1, 0) for b in blocks]
        for b, x in zip(blocks, out):
            att_out[block(b), :] = x.astype(BF16)

    def attend_and_send(i):
        attend([seq_at(2 * i + 1), seq_at(2 * i + 2)])
        att(2 * i + 1).start()
        att(2 * i + 2).start()

    each(0, 7, attend_and_send)
    attend([seq_at(15), here.seq])
    att(15).start()
    own_att.start()
    for j in range(8):
        from_x(j % 2, j).wait_recv()
        to_core(2, j).start()
    for y_hi in range(4):
        own_grads(y_hi).start()
        each(1, NX, lambda d: grads(d, y_hi).start())
    for i in (0, 3, 1, 2):
        for j in range(8):
            to_core(i, j).wait_recv()

    def project(head):
        d_out[head] = jnp.dot(g_ref[...], w_all[head % 2, head // 2], preferred_element_type=F32).astype(BF16)

    def project_and_send(d):
        project(seq_at(d))
        d_att(d).start()

    each(1, 16, project_and_send)
    project(here.seq)
    own_d.start()

    own_att.wait()
    each(1, 16, lambda d: att(d).wait_recv())
    att_copy = pltpu.make_async_copy(mine, att_ref, own_sem.at[5])
    att_copy.start()
    for part in range(2):
        att_x(0, part).start()
        att_x(1, 1 - part).start()
    for way in range(2):
        att_x(way, way).wait_recv()
        att_onward(way).start()
    for way in range(2):
        att_x(way, 1 - way).wait_recv()
    for way in range(2):
        att_onward(way).wait()
    for y_hi in range(4):
        own_grads(y_hi).wait()
        each(1, NX, lambda d: grads(d, y_hi).wait())
    own_d.wait()
    each(1, 16, lambda d: d_att(d).wait())
    att_copy.wait()

    for a, (src, dst) in enumerate(pairs):
        each(1, 16, lambda d: moved(src, dst, a, d).wait_send())
    each(1, 16, lambda d: att(d).wait_send())
    each(1, NZ, lambda d: along_z(d).wait_send())
    for way in range(2):
        for k in range(4):
            along_y(way, k).wait_send()
        for j in range(8):
            along_x(way, j).wait_send()
        for part in range(2):
            att_x(way, part).wait_send()
    for j in range(8):
        from_x(j % 2, j).wait_send()
        for i in range(4):
            to_core(i, j).wait_send()


def outward(ids, q, k, v, g, w):
    any_ = pl.BlockSpec(memory_space=pl.ANY)
    dma = pltpu.SemaphoreType.DMA
    return pl.pallas_call(
        outward_kernel,
        out_shape=(BLOCKED,) * 3
        + (
            FLAT,
            PROBS,
            jax.ShapeDtypeStruct((ROWS, WIDTH), BF16),
            jax.ShapeDtypeStruct((NX, ROWS, WIDTH), BF16),
            jax.ShapeDtypeStruct((NX, ROWS, 4 * HEAD), BF16),
        ),
        in_specs=[pl.BlockSpec(memory_space=pltpu.SMEM)] + [any_] * 3 + [VMEM] * 2,
        out_specs=(VMEM,) * 5 + (any_,) * 3,
        scratch_shapes=[
            pltpu.VMEM((2, NZ, WIDTH, HEAD), BF16),
            pltpu.VMEM((SEQ_LEN, HEAD), BF16),
            pltpu.VMEM((HEADS, ROWS, HEAD), BF16),
            dma((5, 16)), dma((5, 16)), dma((6,)), dma((NZ,)), dma((NZ,)), dma((2, 4)), dma((2, 4)),
            dma((2, 8)), dma((2, 8)), dma((8,)), dma((8,)), dma((4, 8)), dma((4, 8)),
            dma((4, 4)), dma((4, 4)), dma((2, 2)), dma((2, 2)), dma((2,)), dma((2,)),
        ],
        compiler_params=pltpu.CompilerParams(
            collective_id=0, has_side_effects=True, vmem_limit_bytes=44 * 2**20
        ),
        name="outward",
    )(ids, q, k, v, g, w)


def backward_kernel(ids_ref, q_ref, k_ref, v_ref, d_ref, probs_ref, dq_ref, dk_ref, dv_ref, dk_sum, dv_sum):
    dk_sum[...] = jnp.zeros_like(dk_sum)
    dv_sum[...] = jnp.zeros_like(dv_sum)

    def some(step):
        blocks = [step * TOGETHER + i for i in range(TOGETHER)]
        at = [listed(ids_ref, b) for b in blocks]
        d = [d_ref[block(b), :] for b in blocks]
        probs = [probs_ref[b] for b in blocks]
        d_probs = [dot(x, gathered(v_ref, i), 1, 1) for x, i in zip(d, at)]
        delta = [jnp.sum(x * y, axis=1, keepdims=True) for x, y in zip(probs, d_probs)]
        d_logits = [(x * (y - z) * SCALE).astype(BF16) for x, y, z in zip(probs, d_probs, delta)]
        dq = [dot(x, gathered(k_ref, i), 1, 0) for x, i in zip(d_logits, at)]
        dk = [dot(x, q_ref[b], 0, 0) for x, b in zip(d_logits, blocks)]
        dv = [dot(x.astype(BF16), y, 0, 0) for x, y in zip(probs, d)]
        for b, x in zip(blocks, dq):
            dq_ref[block(b), :] = x.astype(BF16)
        for i, x, y in zip(at, dk, dv):
            for s in range(SLOTS):
                dk_sum[block(i[s]), :] += x[s * BLOCK : (s + 1) * BLOCK]
                dv_sum[block(i[s]), :] += y[s * BLOCK : (s + 1) * BLOCK]

    each(0, SEQ_LEN // BLOCK // TOGETHER, some)
    dk_ref[...] = dk_sum[...].astype(BF16)
    dv_ref[...] = dv_sum[...].astype(BF16)


def backward(ids, q, k, v, d, probs):
    return pl.pallas_call(
        backward_kernel,
        out_shape=(FLAT,) * 3,
        in_specs=[pl.BlockSpec(memory_space=pltpu.SMEM)] + [VMEM] * 5,
        out_specs=(VMEM,) * 3,
        scratch_shapes=[pltpu.VMEM((SEQ_LEN, HEAD), F32)] * 2,
        compiler_params=pltpu.CompilerParams(vmem_limit_bytes=32 * 2**20),
        name="backward",
    )(ids, q, k, v, d, probs)


def collect_kernel(
    qh_ref, kh_ref, vh_ref, att4, g4, dq_ref, dk_ref, dv_ref, gw_ref,
    product, c_out, c_in, y_out, y_in, z_out, z_in, last_out, last_in,
    a_send, a_recv, own_sem, c_send, c_recv, y_send, y_recv, z_send, z_recv,
):
    here = Place()
    others = [here.other_core()]
    for d in range(1, 4):
        for y_lo in range(2):
            others.append((here.dp_of(y_hi=(here.y_hi + d) % 4), 2 * here.z + y_lo))
    greet(pltpu.get_barrier_semaphore(), here, others)

    def moved(src, dst, a, d):
        to = (here.seq + d) % 16
        return remote(
            src.at[rows(to), :], dst.at[:, cols(here.seq)], a_send.at[a, d], a_recv.at[a, d], here.at_seq(to)
        )

    def kept(src, dst, a):
        return pltpu.make_async_copy(src.at[rows(here.seq), :], dst.at[:, cols(here.seq)], own_sem.at[a])

    pairs = ((qh_ref, dq_ref), (kh_ref, dk_ref), (vh_ref, dv_ref))
    order = [(0, OTHER_Y), (0, SAME_Y), (1, SAME_Y), (2, SAME_Y), (1, OTHER_Y), (2, OTHER_Y)]
    queue = Queue((moved, *pairs[a], a, d) for a, ds in order for d in ds)
    queue.start(12)
    for a, (src, dst) in enumerate(pairs):
        kept(src, dst, a).start()

    def multiply(h):
        a = att4[:, :, cols(h)].reshape(NX * ROWS, HEAD)
        total = lax.dot_general(
            a, g4[...].reshape(NX * ROWS, 4 * HEAD), (((0,), (0,)), ((), ())), preferred_element_type=F32
        )
        product[h] = total
        c_out[h] = total.astype(BF16)

    each(0, HEADS, multiply)

    def half_rows(core):
        return pl.ds(pl.multiple_of(core * 64, 64), 64)

    to_core = remote(
        c_out.at[:, half_rows(1 - here.core), :], c_in, c_send.at[0], c_recv.at[0], here.other_core()
    )
    to_core.start()
    to_core.wait()

    def add_core(h):
        total = product[h, half_rows(here.core), :] + c_in[h].astype(F32)
        for y_hi in range(4):
            y_out[y_hi * 2 + h % 2, h // 2] = total[:, y_hi * HEAD : (y_hi + 1) * HEAD].astype(BF16)

    each(0, HEADS, add_core)

    def along_y(d):
        y = (here.y + d) % NY
        return remote(y_out.at[y], y_in.at[d], y_send.at[d], y_recv.at[d], here.at_y(y))

    each(1, NY, lambda d: along_y(d).start())
    queue.start(17)
    each(1, NY, lambda d: along_y(d).wait())

    def add_y(z):
        total = y_out[here.y, z].astype(F32)
        for d in range(1, NY):
            total += y_in[d, z].astype(F32)
        z_out[z] = total.astype(BF16)

    each(0, NZ, add_y)

    def along_z(d):
        z = (here.z + d) % NZ
        return remote(z_out.at[z], z_in.at[d], z_send.at[d], z_recv.at[d], here.at_z(z))

    each(1, NZ, lambda d: along_z(d).start())
    queue.start(16)
    each(1, NZ, lambda d: along_z(d).wait())
    total = z_out[here.z].astype(F32)
    for d in range(1, NZ):
        total += z_in[d].astype(F32)
    last_out[...] = total
    swap = remote(last_out, last_in, c_send.at[1], c_recv.at[1], here.other_core())
    swap.start()
    swap.wait()
    first = here.core == 0
    top = jnp.where(first, last_out[...], last_in[...])
    bottom = jnp.where(first, last_in[...], last_out[...])
    gw_ref[:64, :] = jnp.where(first, top[:, :64], top[:, 64:])
    gw_ref[64:, :] = jnp.where(first, bottom[:, :64], bottom[:, 64:])

    for a, (src, dst) in enumerate(pairs):
        kept(src, dst, a).wait()
        each(1, 16, lambda d: moved(src, dst, a, d).wait())


def collect(dq, dk, dv, att4, g4):
    flat = jax.ShapeDtypeStruct((ROWS, WIDTH), BF16)
    any_, vmem = pl.BlockSpec(memory_space=pl.ANY), pl.BlockSpec(memory_space=pltpu.VMEM)
    dma = pltpu.SemaphoreType.DMA
    return pl.pallas_call(
        collect_kernel,
        out_shape=(flat,) * 3 + (jax.ShapeDtypeStruct((HEAD, 64), F32),),
        in_specs=[any_] * 3 + [vmem] * 2,
        out_specs=(any_,) * 3 + (vmem,),
        scratch_shapes=[
            pltpu.VMEM((HEADS, HEAD, 4 * HEAD), F32),
            pltpu.VMEM((HEADS, HEAD, 4 * HEAD), BF16),
            pltpu.VMEM((HEADS, 64, 4 * HEAD), BF16),
            pltpu.VMEM((NY, NZ, 64, HEAD), BF16),
            pltpu.VMEM((NY, NZ, 64, HEAD), BF16),
            pltpu.VMEM((NZ, 64, HEAD), BF16),
            pltpu.VMEM((NZ, 64, HEAD), BF16),
            pltpu.VMEM((64, HEAD), F32),
            pltpu.VMEM((64, HEAD), F32),
            dma((3, 16)), dma((3, 16)), dma((3,)), dma((2,)), dma((2,)),
            dma((NY,)), dma((NY,)), dma((NZ,)), dma((NZ,)),
        ],
        compiler_params=pltpu.CompilerParams(
            collective_id=1, has_side_effects=True, vmem_limit_bytes=40 * 2**20
        ),
        name="collect",
    )(dq, dk, dv, att4, g4)


def in_blocks(flat):
    return flat.reshape(ROWS // BLOCK, BLOCK, WIDTH)


def local(query_rows, key_rows, value_rows, out_weight, grad_out, block_list):
    ids = block_list[0]
    q, k, v, d, probs, att, att4, g4 = outward(
        ids, in_blocks(query_rows), in_blocks(key_rows), in_blocks(value_rows), grad_out[0], out_weight
    )
    dq, dk, dv = backward(ids, q, k, v, d, probs)
    dq, dk, dv, grad_weight = collect(dq, dk, dv, att4, g4)
    return (att[None], dq[None], dk[None], dv[None], grad_weight)


def solution(mesh):
    return jax.shard_map(
        local,
        mesh=mesh,
        in_specs=(
            P("dp", "seq", None),
            P("dp", "seq", None),
            P("dp", "seq", None),
            P("seq", "dp"),
            P("dp", "seq", None),
            P("dp", None, None),
        ),
        out_specs=(
            P("dp", "seq", None),
            P("dp", "seq", None),
            P("dp", "seq", None),
            P("dp", "seq", None),
            P("seq", "dp"),
        ),
        check_vma=False,
    )
```

time: 232 us -> 180 us (0.78); the launches traced: 231 us -> 177 us
  Pallas kernels: 222 us -> 164 us
  local copies, waits for them, and re-layouts: 8.91 us -> 11.8 us
    pallas_call x3, Pallas kernels: 222 us -> 164 us  [the longest x1 96.1 us: outward(): pl.pallas_call(outward_kernel, out_shape=(BLOCKED,) * 3 + (FLAT, PROBS, j...]
    unnamed x21 -> x17, local copies, waits for them, and re-layouts: 8.91 us -> 11.8 us
where the time goes in v2:
time: 180 us; the launch traced here: 177 us
  Pallas kernels  164 us (91%)
  local copies, waits for them, and re-layouts  11.8 us (7%)
    pallas_call x1, Pallas kernels, outward(): pl.pallas_call(outward_kernel, out_shape=(BLOCKED,) * 3 + (FLAT, PROBS, j...  96.1 us
    pallas_call x1, Pallas kernels, collect(): pl.pallas_call(collect_kernel, out_shape=(flat,) * 3 + (jax.ShapeDtypeStr...  59.7 us
    unnamed x17, local copies, waits for them, and re-layouts  11.8 us
    pallas_call x1, Pallas kernels, backward(): pl.pallas_call(backward_kernel, out_shape=(FLAT,) * 3, in_specs=[pl.Block...  8.33 us

profile of v2, /device:TPU:6, one launch (start us, length us, event | category | flops | bytes accessed | tf_op | source)
XLA Modules:
  0.0 176.6 jit_solution(9538223472378910473)
XLA Ops:
  0.6 0.8 copy.11
  1.4 0.8 copy.12.w_ref
  2.2 0.0 copy-start.1
  2.2 1.0 copy-done.1
  3.3 0.0 copy-start.2
  3.3 1.0 copy-done.2
  4.3 0.0 copy-start.3
  4.3 1.0 copy-done.3
  5.4 0.0 copy-start.4
  5.4 1.0 copy-done.4
  6.4 96.1 %outward.1 = (bf16[32,64,128]{2,1,0:T(8,128)(2,1)S(1)}, bf16[32,64,128]{2,1,0:T(8,128)(2,1)S(1)}, bf16[32,64,128]{2,1,0:T(8,128)(2,1)S(1)}, bf16[2048,128]{1,0:T...) custom-call(s32[32,8]{1,0:T(8,128)S(1)} %bitcast.17, ...), custom_call_target="tpu_custom_call" | custom-call | tf_op jit(solution)/shard_map/outward/pallas_call | solution.py:353
  102.5 0.0 copy-start
  102.5 2.2 %copy-done = f32[32,64,512]{2,1,0:T(8,128)S(1)} copy-done((f32[32,64,512]{2,1,0:T(8,128)S(1)}, f32[32,64,512]{2,1,0:T(8,128)}, u32[]{:S(2)}) %copy-start) | copy-done | bytes 4194328
  104.7 8.3 %backward.1 = (bf16[2048,128]{1,0:T(8,128)(2,1)S(1)}, bf16[2048,128]{1,0:T(8,128)(2,1)S(1)}, bf16[2048,128]{1,0:T(8,128)(2,1)S(1)}) custom-call(s32[32,8]{1,0:T(8,128)S(1)} %bitcast.18, bf16[32,64,128]{2,1,0:T(8,128)(2,1)S(1)} %get-tuple-element.21.q_ref, bf16[32,64,128]{2,1,0:T(8,128)(2,1)S(1)} %get-tuple-element.22.k_ref, ...), custom_call_target="tpu_custom_call" | custom-call | tf_op jit(solution)/shard_map/backward/pallas_call | solution.py:408
  113.1 59.7 %collect.1 = (bf16[128,2048]{1,0:T(8,128)(2,1)S(1)}, bf16[128,2048]{1,0:T(8,128)(2,1)S(1)}, bf16[128,2048]{1,0:T(8,128)(2,1)S(1)}, f32[128,64]{1,0:T(8,128)S(1)}) custom-call(bf16[2048,128]{1,0:T(8,128)(2,1)S(1)} %get-tuple-element.26.qh_ref, bf16[2048,128]{1,0:T(8,128)(2,1)S(1)} %get-tuple-element.27.kh_ref, ...), custom_call_target="tpu_custom_call" | custom-call | tf_op jit(solution)/shard_map/collect/pallas_call | solution.py:518
  172.8 0.7 copy.13
  173.5 0.8 copy.18
  174.3 0.8 copy.19
  175.0 0.8 copy.20
  175.8 0.8 copy.21
Async XLA Ops:
  2.2 1.1 copy-start.1
  3.3 1.0 copy-start.2
  4.3 1.0 copy-start.3
  5.4 1.0 copy-start.4
  102.5 2.2 %copy-start = (f32[32,64,512]{2,1,0:T(8,128)S(1)}, f32[32,64,512]{2,1,0:T(8,128)}, u32[]{:S(2)}) copy-start(f32[32,64,512]{2,1,0:T(8,128)} %get-tuple-element.25.probs_ref) | copy-start | bytes 12582916

commit v3 on v2

--- a/solution.py
+++ b/solution.py
@@ -109,33 +109,39 @@
 TOGETHER = 4
 
 
+def fixed(b):
+    return [(b + 31) % 32, b, (b + 1) % 32, 0, 31]
+
+
 def listed(ids_ref, b):
-    return [ids_ref[b, s] for s in range(SLOTS)]
+    return fixed(b) + [ids_ref[b, s] for s in range(5, SLOTS)]
 
 
 def gathered(ref, at):
     return jnp.concatenate([ref[i] for i in at], axis=0)
 
 
-FLAT = jax.ShapeDtypeStruct((SEQ_LEN, HEAD), BF16)
-BLOCKED = jax.ShapeDtypeStruct((SEQ_LEN // BLOCK, BLOCK, HEAD), BF16)
-PROBS = jax.ShapeDtypeStruct((SEQ_LEN // BLOCK, BLOCK, SLOTS * BLOCK), F32)
 VMEM = pl.BlockSpec(memory_space=pltpu.VMEM)
 
 
-def outward_kernel(
-    ids_ref, q_ref, k_ref, v_ref, g_ref, w_ref, qh_ref, kh_ref, vh_ref, dh_ref, probs_ref, att_ref, att4, g4,
-    w_all, att_out, d_out, a_send, a_recv, own_sem, z_send, z_recv, y_send, y_recv, x_send, x_recv,
+def layer_kernel(
+    ids_ref, drawn_ref, q_ref, k_ref, v_ref, g_ref, w_ref, att_ref, dq_ref, dk_ref, dv_ref, gw_ref,
+    qh_ref, kh_ref, vh_ref, dh_ref, probs_ref, att4, g4, w_all, att_out, d_out, q_out, k_out, v_out,
+    k_sum, v_sum, k_drawn, v_drawn, product, p_out, p_in, y_out, y_in, z_out, z_in, last_out, last_in,
+    a_send, a_recv, own_sem, z_send, z_recv, y_send, y_recv, x_send, x_recv,
     f_send, f_recv, c_send, c_recv, g_send, g_recv, m_send, m_recv, n_send, n_recv,
+    b_send, b_recv, own_back, p_send, p_recv, s_send, s_recv, t_send, t_recv,
 ):
     here = Place()
     up = here.at_y((here.y + 1) % NY)
     down = here.at_y((here.y + NY - 1) % NY)
     right = here.at_x((here.x + 1) % NX)
     left = here.at_x((here.x + NX - 1) % NX)
-    far_y = here.at_y((here.y + NY + 2 * here.y_lo - 1) % NY)
-    others = [here.at_x((here.x + d) % NX) for d in range(1, NX)]
-    greet(pltpu.get_barrier_semaphore(), here, [far_y, here.other_core()] + others)
+    others = [here.other_core()] + [here.at_x((here.x + d) % NX) for d in range(1, NX)]
+    for d in range(1, 4):
+        for y_lo in range(2):
+            others.append((here.dp_of(y_hi=(here.y_hi + d) % 4), 2 * here.z + y_lo))
+    greet(pltpu.get_barrier_semaphore(), here, others)
     mine = att4.at[here.x]
 
     def seq_at(d):
@@ -309,6 +315,56 @@
     project(here.seq)
     own_d.start()
 
+    def returned(src, dst, a, d):
+        to = seq_at(d)
+        return remote(
+            src.at[rows(to), :], dst.at[:, cols(here.seq)], b_send.at[a, d], b_recv.at[a, d], here.at_seq(to)
+        )
+
+    def retained(src, dst, a):
+        return pltpu.make_async_copy(src.at[rows(here.seq), :], dst.at[:, cols(here.seq)], own_back.at[a])
+
+    def cleared(step):
+        k_sum[block(step), :] = jnp.zeros((BLOCK, HEAD), F32)
+        v_sum[block(step), :] = jnp.zeros((BLOCK, HEAD), F32)
+
+    each(0, SEQ_LEN // BLOCK, cleared)
+
+    def add(total, place, terms):
+        total[block(place), :] += terms
+
+    def backward(chunks):
+        blocks = [2 * c + i for c in chunks for i in range(2)]
+        at = [listed(ids_ref, b) for b in blocks]
+        d = [dh_ref[block(b), :] for b in blocks]
+        probs = [probs_ref[b] for b in blocks]
+        d_probs = [dot(x, gathered(vh_ref, i), 1, 1) for x, i in zip(d, at)]
+        delta = [jnp.sum(x * y, axis=1, keepdims=True) for x, y in zip(probs, d_probs)]
+        d_logits = [(x * (y - z) * SCALE).astype(BF16) for x, y, z in zip(probs, d_probs, delta)]
+        dq = [dot(x, gathered(kh_ref, i), 1, 0) for x, i in zip(d_logits, at)]
+        for b, x in zip(blocks, dq):
+            q_out[block(b), :] = x.astype(BF16)
+        dk = [dot(x, qh_ref[b], 0, 0) for x, b in zip(d_logits, blocks)]
+        dv = [dot(x.astype(BF16), y, 0, 0) for x, y in zip(probs, d)]
+        for total, drawn, terms in ((k_sum, k_drawn, dk), (v_sum, v_drawn, dv)):
+            for b, x in zip(blocks, terms):
+                for s in range(3):
+                    add(total, fixed(b)[s], x[s * BLOCK : (s + 1) * BLOCK])
+                for s in range(5, SLOTS):
+                    drawn[block((s - 5) * 32 + b), :] = x[s * BLOCK : (s + 1) * BLOCK]
+            for s in (3, 4):
+                add(total, fixed(0)[s], sum(x[s * BLOCK : (s + 1) * BLOCK] for x in terms))
+
+    def chunk_from(d):
+        return (here.seq + 16 - d) % 16
+
+    def backward_and_send(i):
+        d_att(2 * i + 1).wait_recv()
+        d_att(2 * i + 2).wait_recv()
+        backward([chunk_from(2 * i + 1), chunk_from(2 * i + 2)])
+        returned(q_out, dq_ref, 0, 15 - 2 * i).start()
+        returned(q_out, dq_ref, 0, 14 - 2 * i).start()
+
     own_att.wait()
     each(1, 16, lambda d: att(d).wait_recv())
     att_copy = pltpu.make_async_copy(mine, att_ref, own_sem.at[5])
@@ -316,23 +372,123 @@
     for part in range(2):
         att_x(0, part).start()
         att_x(1, 1 - part).start()
+    own_d.wait()
+    each(0, 4, backward_and_send)
     for way in range(2):
         att_x(way, way).wait_recv()
         att_onward(way).start()
+    each(4, 7, backward_and_send)
+    d_att(15).wait_recv()
+    backward([chunk_from(15), here.seq])
+    returned(q_out, dq_ref, 0, 1).start()
+    retained(q_out, dq_ref, 0).start()
+
     for way in range(2):
         att_x(way, 1 - way).wait_recv()
     for way in range(2):
-        att_onward(way).wait()
+        att_onward(way).wait_recv()
     for y_hi in range(4):
         own_grads(y_hi).wait()
-        each(1, NX, lambda d: grads(d, y_hi).wait())
-    own_d.wait()
-    each(1, 16, lambda d: d_att(d).wait())
-    att_copy.wait()
+        each(1, NX, lambda d: grads(d, y_hi).wait_recv())
+
+    def multiply(h):
+        a = att4[:, :, cols(h)].reshape(NX * ROWS, HEAD)
+        total = lax.dot_general(
+            a, g4[...].reshape(NX * ROWS, 4 * HEAD), (((0,), (0,)), ((), ())), preferred_element_type=F32
+        )
+        product[h] = total
+        p_out[h] = total.astype(BF16)
+
+    each(0, HEADS, multiply)
+
+    def half_rows(core):
+        return pl.ds(pl.multiple_of(core * 64, 64), 64)
+
+    to_half = remote(
+        p_out.at[:, half_rows(1 - here.core), :], p_in, p_send.at[0], p_recv.at[0], here.other_core()
+    )
+    to_half.start()
+
+    drawn = drawn_ref[...]
+    hits = (lax.broadcasted_iota(jnp.int32, (32, 96), 0) == jnp.broadcast_to(drawn, (32, 96))).astype(F32).astype(BF16)
+    hits = jnp.concatenate([hits, hits], axis=1)
+
+    def gather_terms(r):
+        for total, terms in ((k_sum, k_drawn), (v_sum, v_drawn)):
+            x = terms[pl.ds(r, 96, stride=BLOCK), :]
+            high = x.astype(BF16)
+            low = (x - high.astype(F32)).astype(BF16)
+            mine_too = jnp.dot(hits, jnp.concatenate([high, low], axis=0), preferred_element_type=F32)
+            at = pl.ds(r, 32, stride=BLOCK)
+            total[at, :] = total[at, :] + mine_too
+
+    def gather_some(i):
+        for r in range(4):
+            gather_terms(4 * i + r)
+
+    each(0, BLOCK // 4, gather_some)
+    k_out[...] = k_sum[...].astype(BF16)
+    v_out[...] = v_sum[...].astype(BF16)
+    order = [(1, SAME_Y), (2, SAME_Y), (1, OTHER_Y), (2, OTHER_Y)]
+    results = ((q_out, dq_ref), (k_out, dk_ref), (v_out, dv_ref))
+    back = Queue((returned, *results[a], a, d) for a, ds in order for d in ds)
+    retained(k_out, dk_ref, 1).start()
+    retained(v_out, dv_ref, 2).start()
+    to_half.wait()
+
+    def add_core(h):
+        total = product[h, half_rows(here.core), :] + p_in[h].astype(F32)
+        for y_hi in range(4):
+            y_out[y_hi * 2 + h % 2, h // 2] = total[:, y_hi * HEAD : (y_hi + 1) * HEAD].astype(BF16)
+
+    each(0, HEADS, add_core)
+
+    def sum_y(d):
+        y = (here.y + d) % NY
+        return remote(y_out.at[y], y_in.at[d], s_send.at[d], s_recv.at[d], here.at_y(y))
+
+    each(1, NY, lambda d: sum_y(d).start())
+    back.start(30)
+    each(1, NY, lambda d: sum_y(d).wait())
+
+    def add_y(z):
+        total = y_out[here.y, z].astype(F32)
+        for d in range(1, NY):
+            total += y_in[d, z].astype(F32)
+        z_out[z] = total.astype(BF16)
+
+    each(0, NZ, add_y)
+
+    def sum_z(d):
+        z = (here.z + d) % NZ
+        return remote(z_out.at[z], z_in.at[d], t_send.at[d], t_recv.at[d], here.at_z(z))
+
+    each(1, NZ, lambda d: sum_z(d).start())
+    each(1, NZ, lambda d: sum_z(d).wait())
+    total = z_out[here.z].astype(F32)
+    for d in range(1, NZ):
+        total += z_in[d].astype(F32)
+    last_out[...] = total
+    swap = remote(last_out, last_in, p_send.at[1], p_recv.at[1], here.other_core())
+    swap.start()
+    swap.wait()
+    first = here.core == 0
+    top = jnp.where(first, last_out[...], last_in[...])
+    bottom = jnp.where(first, last_in[...], last_out[...])
+    gw_ref[:64, :] = jnp.where(first, top[:, :64], top[:, 64:])
+    gw_ref[64:, :] = jnp.where(first, bottom[:, :64], bottom[:, 64:])
+
+    for a, (src, dst) in enumerate(results):
+        retained(src, dst, a).wait()
+        each(1, 16, lambda d: returned(src, dst, a, d).wait())
 
     for a, (src, dst) in enumerate(pairs):
         each(1, 16, lambda d: moved(src, dst, a, d).wait_send())
     each(1, 16, lambda d: att(d).wait_send())
+    each(1, 16, lambda d: d_att(d).wait_send())
+    att_copy.wait()
+    for y_hi in range(4):
+        each(1, NX, lambda d: grads(d, y_hi).wait_send())
     each(1, NZ, lambda d: along_z(d).wait_send())
     for way in range(2):
         for k in range(4):
@@ -341,186 +497,41 @@
             along_x(way, j).wait_send()
         for part in range(2):
             att_x(way, part).wait_send()
+        att_onward(way).wait_send()
     for j in range(8):
         from_x(j % 2, j).wait_send()
         for i in range(4):
             to_core(i, j).wait_send()
 
 
-def outward(ids, q, k, v, g, w):
+def layer(ids, drawn, q, k, v, g, w):
     any_ = pl.BlockSpec(memory_space=pl.ANY)
     dma = pltpu.SemaphoreType.DMA
+    flat = jax.ShapeDtypeStruct((ROWS, WIDTH), BF16)
+    by_head, by_block = (SEQ_LEN, HEAD), (SEQ_LEN // BLOCK, BLOCK, HEAD)
     return pl.pallas_call(
-        outward_kernel,
-        out_shape=(BLOCKED,) * 3
-        + (
-            FLAT,
-            PROBS,
-            jax.ShapeDtypeStruct((ROWS, WIDTH), BF16),
-            jax.ShapeDtypeStruct((NX, ROWS, WIDTH), BF16),
-            jax.ShapeDtypeStruct((NX, ROWS, 4 * HEAD), BF16),
-        ),
-        in_specs=[pl.BlockSpec(memory_space=pltpu.SMEM)] + [any_] * 3 + [VMEM] * 2,
-        out_specs=(VMEM,) * 5 + (any_,) * 3,
+        layer_kernel,
+        out_shape=(flat,) * 4 + (jax.ShapeDtypeStruct((HEAD, 64), F32),),
+        in_specs=[pl.BlockSpec(memory_space=pltpu.SMEM), VMEM] + [any_] * 3 + [VMEM] * 2,
+        out_specs=(any_,) * 4 + (VMEM,),
         scratch_shapes=[
+            pltpu.VMEM(by_block, BF16),
+            pltpu.VMEM(by_block, BF16),
+            pltpu.VMEM(by_block, BF16),
+            pltpu.VMEM(by_head, BF16),
+            pltpu.VMEM((SEQ_LEN // BLOCK, BLOCK, SLOTS * BLOCK), F32),
+            pltpu.VMEM((NX, ROWS, WIDTH), BF16),
+            pltpu.VMEM((NX, ROWS, 4 * HEAD), BF16),
             pltpu.VMEM((2, NZ, WIDTH, HEAD), BF16),
-            pltpu.VMEM((SEQ_LEN, HEAD), BF16),
+            pltpu.VMEM(by_head, BF16),
             pltpu.VMEM((HEADS, ROWS, HEAD), BF16),
-            dma((5, 16)), dma((5, 16)), dma((6,)), dma((NZ,)), dma((NZ,)), dma((2, 4)), dma((2, 4)),
-            dma((2, 8)), dma((2, 8)), dma((8,)), dma((8,)), dma((4, 8)), dma((4, 8)),
-            dma((4, 4)), dma((4, 4)), dma((2, 2)), dma((2, 2)), dma((2,)), dma((2,)),
-        ],
-        compiler_params=pltpu.CompilerParams(
-            collective_id=0, has_side_effects=True, vmem_limit_bytes=44 * 2**20
-        ),
-        name="outward",
-    )(ids, q, k, v, g, w)
-
-
-def backward_kernel(ids_ref, q_ref, k_ref, v_ref, d_ref, probs_ref, dq_ref, dk_ref, dv_ref, dk_sum, dv_sum):
-    dk_sum[...] = jnp.zeros_like(dk_sum)
-    dv_sum[...] = jnp.zeros_like(dv_sum)
-
-    def some(step):
-        blocks = [step * TOGETHER + i for i in range(TOGETHER)]
-        at = [listed(ids_ref, b) for b in blocks]
-        d = [d_ref[block(b), :] for b in blocks]
-        probs = [probs_ref[b] for b in blocks]
-        d_probs = [dot(x, gathered(v_ref, i), 1, 1) for x, i in zip(d, at)]
-        delta = [jnp.sum(x * y, axis=1, keepdims=True) for x, y in zip(probs, d_probs)]
-        d_logits = [(x * (y - z) * SCALE).astype(BF16) for x, y, z in zip(probs, d_probs, delta)]
-        dq = [dot(x, gathered(k_ref, i), 1, 0) for x, i in zip(d_logits, at)]
-        dk = [dot(x, q_ref[b], 0, 0) for x, b in zip(d_logits, blocks)]
-        dv = [dot(x.astype(BF16), y, 0, 0) for x, y in zip(probs, d)]
-        for b, x in zip(blocks, dq):
-            dq_ref[block(b), :] = x.astype(BF16)
-        for i, x, y in zip(at, dk, dv):
-            for s in range(SLOTS):
-                dk_sum[block(i[s]), :] += x[s * BLOCK : (s + 1) * BLOCK]
-                dv_sum[block(i[s]), :] += y[s * BLOCK : (s + 1) * BLOCK]
-
-    each(0, SEQ_LEN // BLOCK // TOGETHER, some)
-    dk_ref[...] = dk_sum[...].astype(BF16)
-    dv_ref[...] = dv_sum[...].astype(BF16)
-
-
-def backward(ids, q, k, v, d, probs):
-    return pl.pallas_call(
-        backward_kernel,
-        out_shape=(FLAT,) * 3,
-        in_specs=[pl.BlockSpec(memory_space=pltpu.SMEM)] + [VMEM] * 5,
-        out_specs=(VMEM,) * 3,
-        scratch_shapes=[pltpu.VMEM((SEQ_LEN, HEAD), F32)] * 2,
-        compiler_params=pltpu.CompilerParams(vmem_limit_bytes=32 * 2**20),
-        name="backward",
-    )(ids, q, k, v, d, probs)
-
-
-def collect_kernel(
-    qh_ref, kh_ref, vh_ref, att4, g4, dq_ref, dk_ref, dv_ref, gw_ref,
-    product, c_out, c_in, y_out, y_in, z_out, z_in, last_out, last_in,
-    a_send, a_recv, own_sem, c_send, c_recv, y_send, y_recv, z_send, z_recv,
-):
-    here = Place()
-    others = [here.other_core()]
-    for d in range(1, 4):
-        for y_lo in range(2):
-            others.append((here.dp_of(y_hi=(here.y_hi + d) % 4), 2 * here.z + y_lo))
-    greet(pltpu.get_barrier_semaphore(), here, others)
-
-    def moved(src, dst, a, d):
-        to = (here.seq + d) % 16
-        return remote(
-            src.at[rows(to), :], dst.at[:, cols(here.seq)], a_send.at[a, d], a_recv.at[a, d], here.at_seq(to)
-        )
-
-    def kept(src, dst, a):
-        return pltpu.make_async_copy(src.at[rows(here.seq), :], dst.at[:, cols(here.seq)], own_sem.at[a])
-
-    pairs = ((qh_ref, dq_ref), (kh_ref, dk_ref), (vh_ref, dv_ref))
-    order = [(0, OTHER_Y), (0, SAME_Y), (1, SAME_Y), (2, SAME_Y), (1, OTHER_Y), (2, OTHER_Y)]
-    queue = Queue((moved, *pairs[a], a, d) for a, ds in order for d in ds)
-    queue.start(12)
-    for a, (src, dst) in enumerate(pairs):
-        kept(src, dst, a).start()
-
-    def multiply(h):
-        a = att4[:, :, cols(h)].reshape(NX * ROWS, HEAD)
-        total = lax.dot_general(
-            a, g4[...].reshape(NX * ROWS, 4 * HEAD), (((0,), (0,)), ((), ())), preferred_element_type=F32
-        )
-        product[h] = total
-        c_out[h] = total.astype(BF16)
-
-    each(0, HEADS, multiply)
-
-    def half_rows(core):
-        return pl.ds(pl.multiple_of(core * 64, 64), 64)
-
-    to_core = remote(
-        c_out.at[:, half_rows(1 - here.core), :], c_in, c_send.at[0], c_recv.at[0], here.other_core()
-    )
-    to_core.start()
-    to_core.wait()
-
-    def add_core(h):
-        total = product[h, half_rows(here.core), :] + c_in[h].astype(F32)
-        for y_hi in range(4):
-            y_out[y_hi * 2 + h % 2, h // 2] = total[:, y_hi * HEAD : (y_hi + 1) * HEAD].astype(BF16)
-
-    each(0, HEADS, add_core)
-
-    def along_y(d):
-        y = (here.y + d) % NY
-        return remote(y_out.at[y], y_in.at[d], y_send.at[d], y_recv.at[d], here.at_y(y))
-
-    each(1, NY, lambda d: along_y(d).start())
-    queue.start(17)
-    each(1, NY, lambda d: along_y(d).wait())
-
-    def add_y(z):
-        total = y_out[here.y, z].astype(F32)
-        for d in range(1, NY):
-            total += y_in[d, z].astype(F32)
-        z_out[z] = total.astype(BF16)
-
-    each(0, NZ, add_y)
-
-    def along_z(d):
-        z = (here.z + d) % NZ
-        return remote(z_out.at[z], z_in.at[d], z_send.at[d], z_recv.at[d], here.at_z(z))
-
-    each(1, NZ, lambda d: along_z(d).start())
-    queue.start(16)
-    each(1, NZ, lambda d: along_z(d).wait())
-    total = z_out[here.z].astype(F32)
-    for d in range(1, NZ):
-        total += z_in[d].astype(F32)
-    last_out[...] = total
-    swap = remote(last_out, last_in, c_send.at[1], c_recv.at[1], here.other_core())
-    swap.start()
-    swap.wait()
-    first = here.core == 0
-    top = jnp.where(first, last_out[...], last_in[...])
-    bottom = jnp.where(first, last_in[...], last_out[...])
-    gw_ref[:64, :] = jnp.where(first, top[:, :64], top[:, 64:])
-    gw_ref[64:, :] = jnp.where(first, bottom[:, :64], bottom[:, 64:])
-
-    for a, (src, dst) in enumerate(pairs):
-        kept(src, dst, a).wait()
-        each(1, 16, lambda d: moved(src, dst, a, d).wait())
-
-
-def collect(dq, dk, dv, att4, g4):
-    flat = jax.ShapeDtypeStruct((ROWS, WIDTH), BF16)
-    any_, vmem = pl.BlockSpec(memory_space=pl.ANY), pl.BlockSpec(memory_space=pltpu.VMEM)
-    dma = pltpu.SemaphoreType.DMA
-    return pl.pallas_call(
-        collect_kernel,
-        out_shape=(flat,) * 3 + (jax.ShapeDtypeStruct((HEAD, 64), F32),),
-        in_specs=[any_] * 3 + [vmem] * 2,
-        out_specs=(any_,) * 3 + (vmem,),
-        scratch_shapes=[
+            pltpu.VMEM(by_head, BF16),
+            pltpu.VMEM(by_head, BF16),
+            pltpu.VMEM(by_head, BF16),
+            pltpu.VMEM(by_head, F32),
+            pltpu.VMEM(by_head, F32),
+            pltpu.VMEM((96 * BLOCK, HEAD), F32),
+            pltpu.VMEM((96 * BLOCK, HEAD), F32),
             pltpu.VMEM((HEADS, HEAD, 4 * HEAD), F32),
             pltpu.VMEM((HEADS, HEAD, 4 * HEAD), BF16),
             pltpu.VMEM((HEADS, 64, 4 * HEAD), BF16),
@@ -530,14 +541,17 @@
             pltpu.VMEM((NZ, 64, HEAD), BF16),
             pltpu.VMEM((64, HEAD), F32),
             pltpu.VMEM((64, HEAD), F32),
+            dma((5, 16)), dma((5, 16)), dma((6,)), dma((NZ,)), dma((NZ,)), dma((2, 4)), dma((2, 4)),
+            dma((2, 8)), dma((2, 8)), dma((8,)), dma((8,)), dma((4, 8)), dma((4, 8)),
+            dma((4, 4)), dma((4, 4)), dma((2, 2)), dma((2, 2)), dma((2,)), dma((2,)),
             dma((3, 16)), dma((3, 16)), dma((3,)), dma((2,)), dma((2,)),
             dma((NY,)), dma((NY,)), dma((NZ,)), dma((NZ,)),
         ],
         compiler_params=pltpu.CompilerParams(
-            collective_id=1, has_side_effects=True, vmem_limit_bytes=40 * 2**20
+            collective_id=0, has_side_effects=True, vmem_limit_bytes=50 * 2**20
         ),
-        name="collect",
-    )(dq, dk, dv, att4, g4)
+        name="layer",
+    )(ids, drawn, q, k, v, g, w)
 
 
 def in_blocks(flat):
@@ -546,11 +560,10 @@
 
 def local(query_rows, key_rows, value_rows, out_weight, grad_out, block_list):
     ids = block_list[0]
-    q, k, v, d, probs, att, att4, g4 = outward(
-        ids, in_blocks(query_rows), in_blocks(key_rows), in_blocks(value_rows), grad_out[0], out_weight
+    drawn = ids[:, 5:].T.reshape(1, 96)
+    att, dq, dk, dv, grad_weight = layer(
+        ids, drawn, in_blocks(query_rows), in_blocks(key_rows), in_blocks(value_rows), grad_out[0], out_weight
     )
-    dq, dk, dv = backward(ids, q, k, v, d, probs)
-    dq, dk, dv, grad_weight = collect(dq, dk, dv, att4, g4)
     return (att[None], dq[None], dk[None], dv[None], grad_weight)
 
 

time: 180 us -> 164 us (0.911)
  the two profiles are of different devices: /device:TPU:6 before, /device:TPU:17 now
where the time goes in v3:
time: 164 us
  Pallas kernels  155 us (95%)
  local copies, waits for them, and re-layouts  8.66 us (5%)
    pallas_call x1, Pallas kernels, layer(): pl.pallas_call(layer_kernel, out_shape=(flat,) * 4 + (jax.ShapeDtypeStruc...  155 us
    unnamed x17, local copies, waits for them, and re-layouts  8.42 us

profile of v3, /device:TPU:17, one launch (start us, length us, event | category | flops | bytes accessed | tf_op | source)
XLA Modules:
  0.0 163.9 jit_solution(3279983063322447236)
XLA Ops:
  0.6 0.0 copy-start.4
  0.6 0.7 copy-done.4
  1.3 0.1 copy.11
  1.4 0.1 slice_bitcast_fusion
  1.5 0.0 copy-start.3
  1.5 0.1 copy.12
  1.6 0.1 reshape.22.drawn_ref
  1.6 0.6 copy-done.3
  2.2 0.1 copy.13.w_ref
  2.3 0.0 copy-start
  2.3 1.0 copy-done
  3.4 0.0 copy-start.1
  3.4 1.0 copy-done.1
  4.4 0.0 copy-start.2
  4.4 1.0 copy-done.2
  5.4 154.6 %layer.1 = (bf16[128,2048]{1,0:T(8,128)(2,1)S(1)}, bf16[128,2048]{1,0:T(8,128)(2,1)S(1)}, bf16[128,2048]{1,0:T(8,128)(2,1)S(1)}, bf16[128,2048]{1,0:T(8,128)(2,1)S(1)}, f32[128,64]{1,0:T(8,128)S(1)}) custom-call(s32[32,8]{1,0:T(8,128)S(1)} %bitcast.19, s32[1,96]{1,0:T(1,128)S(1)} %reshape.22.drawn_ref, bf16[2,64,2048]{2,1,0:T(8,128)(2,1)S(1)} %bitcast.11, ...), custom_call_target="tpu_custom_call" | custom-call | tf_op jit(solution)/shard_map/layer/pallas_call | solution.py:512
  160.1 0.7 copy.14
  160.8 0.8 copy.19
  161.6 0.8 copy.20
  162.4 0.8 copy.21
  163.1 0.8 copy.22
Async XLA Ops:
  0.6 0.7 copy-start.4
  1.5 0.7 copy-start.3
  2.3 1.1 copy-start
  3.4 1.0 copy-start.1
  4.4 1.0 copy-start.2

commit v4 on v3

--- a/solution.py
+++ b/solution.py
@@ -126,7 +126,7 @@
 
 def layer_kernel(
     ids_ref, drawn_ref, q_ref, k_ref, v_ref, g_ref, w_ref, att_ref, dq_ref, dk_ref, dv_ref, gw_ref,
-    qh_ref, kh_ref, vh_ref, dh_ref, probs_ref, att4, g4, w_all, att_out, d_out, q_out, k_out, v_out,
+    qh_ref, kh_ref, vh_ref, dh_ref, probs_ref, mine, att4, g4, w_all, att_out, d_out, q_out, k_out, v_out,
     k_sum, v_sum, k_drawn, v_drawn, product, p_out, p_in, y_out, y_in, z_out, z_in, last_out, last_in,
     a_send, a_recv, own_sem, z_send, z_recv, y_send, y_recv, x_send, x_recv,
     f_send, f_recv, c_send, c_recv, g_send, g_recv, m_send, m_recv, n_send, n_recv,
@@ -141,8 +141,10 @@
     for d in range(1, 4):
         for y_lo in range(2):
             others.append((here.dp_of(y_hi=(here.y_hi + d) % 4), 2 * here.z + y_lo))
+    for core in range(2):
+        others.append((here.dp_of(x=here.z % 4, core=core), 2 * (2 * here.x + 1 - here.z // 4) + here.y_lo))
+        others.append((here.dp_of(x=here.z // 2, core=core), 2 * ((1 - here.z % 2) * 4 + here.x) + here.y_lo))
     greet(pltpu.get_barrier_semaphore(), here, others)
-    mine = att4.at[here.x]
 
     def seq_at(d):
         return (here.seq + d) % 16
@@ -194,17 +196,10 @@
         along_x(1, j).start()
         to_core(0, j).start()
 
-    def grads(d, y_hi):
-        x = (here.x + d) % NX
-        return remote(
-            g_ref.at[:, cols(y_hi * NX + x)], g4.at[here.x, :, cols(y_hi)], g_send.at[d, y_hi], g_recv.at[d, y_hi],
-            here.at_x(x),
-        )
-
-    def own_grads(y_hi):
-        return pltpu.make_async_copy(
-            g_ref.at[:, cols(y_hi * NX + here.x)], g4.at[here.x, :, cols(y_hi)], g_send.at[0, y_hi]
-        )
+    def grads(d):
+        return remote(g_ref, g4.at[here.x], g_send.at[d], g_recv.at[d], here.at_x((here.x + d) % NX))
+
+    own_grads = pltpu.make_async_copy(g_ref, g4.at[here.x], g_send.at[0])
 
     def att(d):
         to = seq_at(d)
@@ -220,16 +215,14 @@
 
     own_d = pltpu.make_async_copy(d_out.at[here.seq], dh_ref.at[rows(here.seq), :], own_sem.at[4])
 
-    def half(part, x):
-        return att4.at[x, :, pl.ds(part * (WIDTH // 2), WIDTH // 2)]
-
-    def att_x(way, part):
-        at = half(part, here.x)
-        return remote(at, at, m_send.at[way, part], m_recv.at[way, part], right if way == 0 else left)
-
-    def att_onward(way):
-        at = half(way, (here.x + (NX - 1 if way == 0 else 1)) % NX)
-        return remote(at, at, n_send.at[way], n_recv.at[way], right if way == 0 else left)
+    def quarter(x):
+        return mine.at[:, pl.ds(pl.multiple_of(x * 4 * HEAD, 4 * HEAD), 4 * HEAD)]
+
+    def att_x(d):
+        x = (here.x + d) % NX
+        return remote(quarter(x), att4.at[here.x], m_send.at[d], m_recv.at[d], here.at_x(x))
+
+    own_att_x = pltpu.make_async_copy(quarter(here.x), att4.at[here.x], m_send.at[0])
 
     pairs = ((q_ref, qh_ref), (k_ref, kh_ref), (v_ref, vh_ref))
     order = [(0, SAME_Y), (1, SAME_Y), (0, OTHER_Y), (1, OTHER_Y), (2, SAME_Y), (2, OTHER_Y)]
@@ -297,9 +290,8 @@
     for j in range(8):
         from_x(j % 2, j).wait_recv()
         to_core(2, j).start()
-    for y_hi in range(4):
-        own_grads(y_hi).start()
-        each(1, NX, lambda d: grads(d, y_hi).start())
+    own_grads.start()
+    each(1, NX, lambda d: grads(d).start())
     for i in (0, 3, 1, 2):
         for j in range(8):
             to_core(i, j).wait_recv()
@@ -369,45 +361,14 @@
     each(1, 16, lambda d: att(d).wait_recv())
     att_copy = pltpu.make_async_copy(mine, att_ref, own_sem.at[5])
     att_copy.start()
-    for part in range(2):
-        att_x(0, part).start()
-        att_x(1, 1 - part).start()
+    own_att_x.start()
+    each(1, NX, lambda d: att_x(d).start())
     own_d.wait()
-    each(0, 4, backward_and_send)
-    for way in range(2):
-        att_x(way, way).wait_recv()
-        att_onward(way).start()
-    each(4, 7, backward_and_send)
+    each(0, 7, backward_and_send)
     d_att(15).wait_recv()
     backward([chunk_from(15), here.seq])
     returned(q_out, dq_ref, 0, 1).start()
     retained(q_out, dq_ref, 0).start()
-
-    for way in range(2):
-        att_x(way, 1 - way).wait_recv()
-    for way in range(2):
-        att_onward(way).wait_recv()
-    for y_hi in range(4):
-        own_grads(y_hi).wait()
-        each(1, NX, lambda d: grads(d, y_hi).wait_recv())
-
-    def multiply(h):
-        a = att4[:, :, cols(h)].reshape(NX * ROWS, HEAD)
-        total = lax.dot_general(
-            a, g4[...].reshape(NX * ROWS, 4 * HEAD), (((0,), (0,)), ((), ())), preferred_element_type=F32
-        )
-        product[h] = total
-        p_out[h] = total.astype(BF16)
-
-    each(0, HEADS, multiply)
-
-    def half_rows(core):
-        return pl.ds(pl.multiple_of(core * 64, 64), 64)
-
-    to_half = remote(
-        p_out.at[:, half_rows(1 - here.core), :], p_in, p_send.at[0], p_recv.at[0], here.other_core()
-    )
-    to_half.start()
 
     drawn = drawn_ref[...]
     hits = (lax.broadcasted_iota(jnp.int32, (32, 96), 0) == jnp.broadcast_to(drawn, (32, 96))).astype(F32).astype(BF16)
@@ -434,30 +395,84 @@
     back = Queue((returned, *results[a], a, d) for a, ds in order for d in ds)
     retained(k_out, dk_ref, 1).start()
     retained(v_out, dv_ref, 2).start()
+    back.start(14)
+
+    own_att_x.wait()
+    own_grads.wait()
+    each(1, NX, lambda d: att_x(d).wait_recv())
+    each(1, NX, lambda d: grads(d).wait_recv())
+
+    def multiply(i):
+        head, y_hi = i // 4, i % 4
+        a = att4[:, :, cols(head)].reshape(NX * ROWS, HEAD)
+        g = g4[:, :, pl.ds(pl.multiple_of(y_hi * 4 * HEAD, 4 * HEAD), 4 * HEAD)].reshape(NX * ROWS, 4 * HEAD)
+        total = dot(a, g, 0, 0)
+        product[i] = total
+        p_out[i] = total.astype(BF16)
+
+    each(0, HEADS, multiply)
+
+    def half_rows(core):
+        return pl.ds(pl.multiple_of(core * 64, 64), 64)
+
+    to_half = remote(
+        p_out.at[:, half_rows(1 - here.core), :], p_in, p_send.at[0], p_recv.at[0], here.other_core()
+    )
+    to_half.start()
+
     to_half.wait()
 
-    def add_core(h):
-        total = product[h, half_rows(here.core), :] + p_in[h].astype(F32)
-        for y_hi in range(4):
-            y_out[y_hi * 2 + h % 2, h // 2] = total[:, y_hi * HEAD : (y_hi + 1) * HEAD].astype(BF16)
+    def add_core(i):
+        head, y_hi = i // 4, i % 4
+        total = product[i, half_rows(here.core), :] + p_in[i].astype(F32)
+        for x in range(NX):
+            slot = (1 - head // 2) * 4 + x
+            y_out[2 * y_hi + head % 2, slot] = total[:, x * HEAD : (x + 1) * HEAD].astype(BF16)
 
     each(0, HEADS, add_core)
 
-    def sum_y(d):
-        y = (here.y + d) % NY
-        return remote(y_out.at[y], y_in.at[d], s_send.at[d], s_recv.at[d], here.at_y(y))
-
-    each(1, NY, lambda d: sum_y(d).start())
-    back.start(30)
-    each(1, NY, lambda d: sum_y(d).wait())
-
-    def add_y(z):
-        total = y_out[here.y, z].astype(F32)
-        for d in range(1, NY):
-            total += y_in[d, z].astype(F32)
+    def half_of(k, way):
+        return slice(None) if k > 0 else pl.ds(4 * way, 4)
+
+    def target(way, k):
+        return (here.y + (4 - k if way == 0 else 4 + k)) % NY
+
+    def sum_y(way, k):
+        part = half_of(k, way)
+        return remote(
+            y_out.at[target(way, k), part], y_in.at[4 * way + k, part], s_send.at[way, k], s_recv.at[way, k],
+            up if way == 0 else down,
+        )
+
+    def next_y(k):
+        for way in range(2):
+            sum_y(way, k - 1).wait_recv()
+            low = 0 if k > 1 else 4 * way
+
+            def add_y(slot):
+                mine_too = y_out[target(way, k), slot].astype(F32)
+                y_out[target(way, k), slot] = (mine_too + y_in[4 * way + k - 1, slot].astype(F32)).astype(BF16)
+
+            each(low, NZ if k > 1 else low + 4, add_y)
+            sum_y(way, k).start()
+
+    sum_y(0, 0).start()
+    sum_y(1, 0).start()
+
+    next_y(1)
+    back.start(5)
+    next_y(2)
+    back.start(5)
+    next_y(3)
+    back.start(6)
+    sum_y(0, 3).wait_recv()
+    sum_y(1, 3).wait_recv()
+
+    def finish_y(z):
+        total = y_out[here.y, z].astype(F32) + y_in[3, z].astype(F32) + y_in[7, z].astype(F32)
         z_out[z] = total.astype(BF16)
 
-    each(0, NZ, add_y)
+    each(0, NZ, finish_y)
 
     def sum_z(d):
         z = (here.z + d) % NZ
@@ -469,12 +484,21 @@
     for d in range(1, NZ):
         total += z_in[d].astype(F32)
     last_out[...] = total
-    swap = remote(last_out, last_in, p_send.at[1], p_recv.at[1], here.other_core())
-    swap.start()
-    swap.wait()
+
+    def to_owner(core):
+        to = (here.dp_of(x=here.z % 4, core=core), 2 * (2 * here.x + 1 - here.z // 4) + here.y_lo)
+        return remote(last_out, last_in.at[here.core], n_send.at[core], n_recv.at[here.core], to)
+
+    def from_owner(core):
+        to = (here.dp_of(x=here.z % 4, core=core), 2 * (2 * here.x + 1 - here.z // 4) + here.y_lo)
+        return remote(last_out, last_in.at[core], n_send.at[core], n_recv.at[core], to)
+
+    for core in range(2):
+        to_owner(core).start()
+    for core in range(2):
+        from_owner(core).wait_recv()
     first = here.core == 0
-    top = jnp.where(first, last_out[...], last_in[...])
-    bottom = jnp.where(first, last_in[...], last_out[...])
+    top, bottom = last_in[0], last_in[1]
     gw_ref[:64, :] = jnp.where(first, top[:, :64], top[:, 64:])
     gw_ref[64:, :] = jnp.where(first, bottom[:, :64], bottom[:, 64:])
 
@@ -487,17 +511,19 @@
     each(1, 16, lambda d: att(d).wait_send())
     each(1, 16, lambda d: d_att(d).wait_send())
     att_copy.wait()
-    for y_hi in range(4):
-        each(1, NX, lambda d: grads(d, y_hi).wait_send())
+    each(1, NX, lambda d: grads(d).wait_send())
+    each(1, NX, lambda d: att_x(d).wait_send())
+    for core in range(2):
+        to_owner(core).wait_send()
+    for way in range(2):
+        for k in range(4):
+            sum_y(way, k).wait_send()
     each(1, NZ, lambda d: along_z(d).wait_send())
     for way in range(2):
         for k in range(4):
             along_y(way, k).wait_send()
         for j in range(8):
             along_x(way, j).wait_send()
-        for part in range(2):
-            att_x(way, part).wait_send()
-        att_onward(way).wait_send()
     for j in range(8):
         from_x(j % 2, j).wait_send()
         for i in range(4):
@@ -512,7 +538,7 @@
     return pl.pallas_call(
         layer_kernel,
         out_shape=(flat,) * 4 + (jax.ShapeDtypeStruct((HEAD, 64), F32),),
-        in_specs=[pl.BlockSpec(memory_space=pltpu.SMEM), VMEM] + [any_] * 3 + [VMEM] * 2,
+        in_specs=[pl.BlockSpec(memory_space=pltpu.SMEM), VMEM] + [pl.BlockSpec(memory_space=pltpu.HBM)] * 3 + [VMEM] * 2,
         out_specs=(any_,) * 4 + (VMEM,),
         scratch_shapes=[
             pltpu.VMEM(by_block, BF16),
@@ -520,8 +546,9 @@
             pltpu.VMEM(by_block, BF16),
             pltpu.VMEM(by_head, BF16),
             pltpu.VMEM((SEQ_LEN // BLOCK, BLOCK, SLOTS * BLOCK), F32),
+            pltpu.VMEM((ROWS, WIDTH), BF16),
+            pltpu.VMEM((NX, ROWS, 4 * HEAD), BF16),
             pltpu.VMEM((NX, ROWS, WIDTH), BF16),
-            pltpu.VMEM((NX, ROWS, 4 * HEAD), BF16),
             pltpu.VMEM((2, NZ, WIDTH, HEAD), BF16),
             pltpu.VMEM(by_head, BF16),
             pltpu.VMEM((HEADS, ROWS, HEAD), BF16),
@@ -540,12 +567,12 @@
             pltpu.VMEM((NZ, 64, HEAD), BF16),
             pltpu.VMEM((NZ, 64, HEAD), BF16),
             pltpu.VMEM((64, HEAD), F32),
-            pltpu.VMEM((64, HEAD), F32),
+            pltpu.VMEM((2, 64, HEAD), F32),
             dma((5, 16)), dma((5, 16)), dma((6,)), dma((NZ,)), dma((NZ,)), dma((2, 4)), dma((2, 4)),
             dma((2, 8)), dma((2, 8)), dma((8,)), dma((8,)), dma((4, 8)), dma((4, 8)),
-            dma((4, 4)), dma((4, 4)), dma((2, 2)), dma((2, 2)), dma((2,)), dma((2,)),
-            dma((3, 16)), dma((3, 16)), dma((3,)), dma((2,)), dma((2,)),
-            dma((NY,)), dma((NY,)), dma((NZ,)), dma((NZ,)),
+            dma((4,)), dma((4,)), dma((4,)), dma((4,)), dma((2,)), dma((2,)),
+            dma((3, 16)), dma((3, 16)), dma((3,)), dma((1,)), dma((1,)),
+            dma((2, 4)), dma((2, 4)), dma((NZ,)), dma((NZ,)),
         ],
         compiler_params=pltpu.CompilerParams(
             collective_id=0, has_side_effects=True, vmem_limit_bytes=50 * 2**20

time: 164 us -> 158 us (0.963)
  the two profiles are of different devices: /device:TPU:17 before, /device:TPU:6 now
where the time goes in v4:
time: 158 us; the launch traced here: 156 us
  Pallas kernels  147 us (93%)
  local copies, waits for them, and re-layouts  8.66 us (5%)
    pallas_call x1, Pallas kernels, layer(): pl.pallas_call(layer_kernel, out_shape=(flat,) * 4 + (jax.ShapeDtypeStruc...  147 us
    unnamed x17, local copies, waits for them, and re-layouts  8.42 us

profile of v4, /device:TPU:6, one launch (start us, length us, event | category | flops | bytes accessed | tf_op | source)
XLA Modules:
  0.0 156.4 jit_solution(14807461075979075601)
XLA Ops:
  0.6 0.0 copy-start.4
  0.6 0.7 copy-done.4
  1.3 0.1 copy.11
  1.4 0.1 slice_bitcast_fusion
  1.5 0.0 copy-start.3
  1.5 0.1 copy.12
  1.6 0.1 reshape.22.drawn_ref
  1.6 0.6 copy-done.3
  2.2 0.1 copy.13.w_ref
  2.3 0.0 copy-start
  2.3 1.0 copy-done
  3.4 0.0 copy-start.1
  3.4 1.0 copy-done.1
  4.4 0.0 copy-start.2
  4.4 1.0 copy-done.2
  5.4 147.1 %layer.1 = (bf16[128,2048]{1,0:T(8,128)(2,1)S(1)}, bf16[128,2048]{1,0:T(8,128)(2,1)S(1)}, bf16[128,2048]{1,0:T(8,128)(2,1)S(1)}, bf16[128,2048]{1,0:T(8,128)(2,1)S(1)}, f32[128,64]{1,0:T(8,128)S(1)}) custom-call(s32[32,8]{1,0:T(8,128)S(1)} %bitcast.19, s32[1,96]{1,0:T(1,128)S(1)} %reshape.22.drawn_ref, bf16[2,64,2048]{2,1,0:T(8,128)(2,1)S(1)} %bitcast.11, ...), custom_call_target="tpu_custom_call" | custom-call | tf_op jit(solution)/shard_map/layer/pallas_call | solution.py:538
  152.5 0.7 copy.14
  153.2 0.8 copy.19
  154.0 0.8 copy.20
  154.8 0.8 copy.21
  155.6 0.8 copy.22
Async XLA Ops:
  0.6 0.7 copy-start.4
  1.5 0.7 copy-start.3
  2.3 1.1 copy-start
  3.4 1.0 copy-start.1
  4.4 1.0 copy-start.2

commit v5 on v4

--- a/solution.py
+++ b/solution.py
@@ -279,13 +279,13 @@
             att_out[block(b), :] = x.astype(BF16)
 
     def attend_and_send(i):
-        attend([seq_at(2 * i + 1), seq_at(2 * i + 2)])
-        att(2 * i + 1).start()
-        att(2 * i + 2).start()
+        attend([seq_at(i + 1), seq_at(15 - i)])
+        att(i + 1).start()
+        att(15 - i).start()
 
     each(0, 7, attend_and_send)
-    attend([seq_at(15), here.seq])
-    att(15).start()
+    attend([seq_at(8), here.seq])
+    att(8).start()
     own_att.start()
     for j in range(8):
         from_x(j % 2, j).wait_recv()
@@ -303,7 +303,12 @@
         project(seq_at(d))
         d_att(d).start()
 
-    each(1, 16, project_and_send)
+    def project_both_ways(i):
+        project_and_send(i + 1)
+        project_and_send(15 - i)
+
+    each(0, 7, project_both_ways)
+    project_and_send(8)
     project(here.seq)
     own_d.start()
 
@@ -351,11 +356,11 @@
         return (here.seq + 16 - d) % 16
 
     def backward_and_send(i):
-        d_att(2 * i + 1).wait_recv()
-        d_att(2 * i + 2).wait_recv()
-        backward([chunk_from(2 * i + 1), chunk_from(2 * i + 2)])
-        returned(q_out, dq_ref, 0, 15 - 2 * i).start()
-        returned(q_out, dq_ref, 0, 14 - 2 * i).start()
+        d_att(i + 1).wait_recv()
+        d_att(15 - i).wait_recv()
+        backward([chunk_from(i + 1), chunk_from(15 - i)])
+        returned(q_out, dq_ref, 0, 15 - i).start()
+        returned(q_out, dq_ref, 0, i + 1).start()
 
     own_att.wait()
     each(1, 16, lambda d: att(d).wait_recv())
@@ -365,9 +370,9 @@
     each(1, NX, lambda d: att_x(d).start())
     own_d.wait()
     each(0, 7, backward_and_send)
-    d_att(15).wait_recv()
-    backward([chunk_from(15), here.seq])
-    returned(q_out, dq_ref, 0, 1).start()
+    d_att(8).wait_recv()
+    backward([chunk_from(8), here.seq])
+    returned(q_out, dq_ref, 0, 8).start()
     retained(q_out, dq_ref, 0).start()
 
     drawn = drawn_ref[...]

time: 158 us -> 154 us (0.975)
  Pallas kernels: 147 us -> 142 us
    pallas_call x1, Pallas kernels: 147 us -> 142 us  [layer(): pl.pallas_call(layer_kernel, out_shape=(flat,) * 4 + (jax.ShapeDtypeStruc...]
where the time goes in v5:
time: 154 us; the launch traced here: 151 us
  Pallas kernels  142 us (92%)
  local copies, waits for them, and re-layouts  8.66 us (6%)
    pallas_call x1, Pallas kernels, layer(): pl.pallas_call(layer_kernel, out_shape=(flat,) * 4 + (jax.ShapeDtypeStruc...  142 us
    unnamed x17, local copies, waits for them, and re-layouts  8.42 us

profile of v5, /device:TPU:6, one launch (start us, length us, event | category | flops | bytes accessed | tf_op | source)
XLA Modules:
  0.0 151.1 jit_solution(7207730273669965195)
XLA Ops:
  0.6 0.0 copy-start.4
  0.6 0.7 copy-done.4
  1.3 0.1 copy.11
  1.4 0.1 slice_bitcast_fusion
  1.5 0.0 copy-start.3
  1.5 0.1 copy.12
  1.6 0.1 reshape.22.drawn_ref
  1.6 0.6 copy-done.3
  2.2 0.1 copy.13.w_ref
  2.3 0.0 copy-start
  2.3 1.0 copy-done
  3.4 0.0 copy-start.1
  3.4 1.0 copy-done.1
  4.4 0.0 copy-start.2
  4.4 1.0 copy-done.2
  5.4 141.8 %layer.1 = (bf16[128,2048]{1,0:T(8,128)(2,1)S(1)}, bf16[128,2048]{1,0:T(8,128)(2,1)S(1)}, bf16[128,2048]{1,0:T(8,128)(2,1)S(1)}, bf16[128,2048]{1,0:T(8,128)(2,1)S(1)}, f32[128,64]{1,0:T(8,128)S(1)}) custom-call(s32[32,8]{1,0:T(8,128)S(1)} %bitcast.19, s32[1,96]{1,0:T(1,128)S(1)} %reshape.22.drawn_ref, bf16[2,64,2048]{2,1,0:T(8,128)(2,1)S(1)} %bitcast.11, ...), custom_call_target="tpu_custom_call" | custom-call | tf_op jit(solution)/shard_map/layer/pallas_call | solution.py:543
  147.3 0.7 copy.14
  148.0 0.8 copy.19
  148.8 0.8 copy.20
  149.6 0.8 copy.21
  150.3 0.8 copy.22
Async XLA Ops:
  0.6 0.7 copy-start.4
  1.5 0.7 copy-start.3
  2.3 1.1 copy-start
  3.4 1.0 copy-start.1
  4.4 1.0 copy-start.2
